TPU v7x, 32 devices: a whole 2x2x4 slice. The times are simulated.
32 devices in a mesh: grp: 2 (over y), smp: 4 (over z), snp: 2 (over x), pair: 2 (over core).
Axes of the slice: x: 2, y: 2, z: 4, core: 2. Of those that a mesh axis runs over, the one named last changes fastest.
Arguments:
- dosage: bfloat16 [16384, 4096], P(('grp', 'smp'), ('snp', 'pair')), parts along dimension 0, may hold values from 0 to 2
- allele_mean: float32 [8192], P('grp'), parts along dimension 0, may hold values from 0.7 to 1.3
- snp_scale: float32 [8192], P('grp'), parts along dimension 0, may hold values from 1.5 to 4.5
- band_next: int32 [128], P('grp'), parts along dimension 0, may hold values from 1 to 2
- ld_prev: float32 [8192, 320], P(('grp', 'smp')), parts along dimension 0, may hold values from -0.95 to 1, as said below
- band_prev: int32 [128], P('grp'), parts along dimension 0, may hold values from 1 to 2
- zscores: float32 [8192, 512], P(('grp', 'smp'), ('snp', 'pair')), parts along dimension 0, may hold values from -22 to 22
- observed: int32 [8192, 8], P(('grp', 'smp'), ('snp', 'pair')), parts along dimension 0, may hold values 0 or 1
Outputs:
- ld_next: float32 [8192, 320], P(('grp', 'snp', 'pair')), parts along dimension 0
- imputed: float32 [8192, 512], P(('grp', 'smp'), ('snp', 'pair')), parts along dimension 0
There are 2 independent parts, one for each index of `grp`. A program takes and returns all parts, laid end to end along the dimension named above; each array names one. Nothing has to cross between parts.
Inputs may be any that keep to these rules, and one draw needn't show every extreme that they name: `ld_prev`: row i holds the band of a symmetric matrix with unit diagonal: entry (i, o) belongs to column 64 * (i // 64) - 128 + o. For every band mask, the masked matrix plus the identity is positive definite.
All inputs are finite; a program needn't handle non-finite values. No bound on the sum of `observed` on one device may be relied on, other than what follows from the above.
Results may differ from a plain program's by a relative error of at most 0.00049.
Values may be sent and summed in bfloat16 or wider, within the bound.
A program may use at most 128 MiB of HBM per device.

v0:
```python
import jax
import jax.numpy as jnp
from jax import lax
from jax.sharding import PartitionSpec as P

TILE = 64
BMAX = 2
TBLK = 64
ITERS = 3


ridge_term = 1.0


def extended_2(cells, sides, width):
    for axis, dim in sides:
        count = lax.axis_size(axis)
        ends = count - 1
        head = lax.slice_in_dim(cells, 0, width, axis=dim)
        tail = lax.slice_in_dim(cells, cells.shape[dim] - width, cells.shape[dim], axis=dim)
        cells = jnp.concatenate(
            [
                lax.ppermute(tail, axis, [(i, (i + 1) % count) for i in range(ends)]),
                cells,
                lax.ppermute(head, axis, [((i + 1) % count, i) for i in range(ends)]),
            ],
            axis=dim,
        )
    return cells


def passed_along(value, axis, by):
    count = lax.axis_size(axis)
    pairs = [(i, i + by) for i in range(count) if 0 <= i + by < count]
    return lax.ppermute(value, axis, pairs)


def band_of(window, tile_size, span):
    local_rows = window.shape[0]
    tile_count = local_rows // tile_size
    blocks = window.reshape(tile_count, tile_size, tile_count + span - 1, tile_size)
    pieces = []
    for offset in range(span):
        diagonal = jnp.diagonal(blocks[:, :, offset : offset + tile_count, :], axis1=0, axis2=2)
        pieces.append(jnp.transpose(diagonal, (2, 0, 1)))
    return jnp.concatenate(pieces, axis=2).reshape(local_rows, span * tile_size)


def tile_table(widths, reach_tiles):
    tile_total = widths.shape[0]
    padded = jnp.pad(widths, reach_tiles)
    columns = []
    for offset in range(-reach_tiles, reach_tiles + 1):
        beside = padded[reach_tiles + offset : reach_tiles + offset + tile_total]
        columns.append(abs(offset) <= jnp.minimum(widths, beside))
    return jnp.stack(columns, axis=1).astype(jnp.float32)


def local_mask(widths, position, tile_count):
    tile_flags = tile_table(widths, BMAX)
    rows_here = lax.dynamic_slice_in_dim(tile_flags, position * tile_count, tile_count, 0)
    return jnp.repeat(jnp.repeat(rows_here, TILE, axis=0), TILE, axis=1)


def transpose_gram(left, right):
    return lax.dot_general(
        left, right, (((0,), (0,)), ((), ())), preferred_element_type=jnp.float32
    )


def band_product(matrix, widened, local_rows, traits_here):
    tile_count = local_rows // TILE
    stacked = widened.reshape(tile_count + 2 * BMAX, TILE, traits_here)
    windows = jnp.concatenate(
        [stacked[offset : offset + tile_count] for offset in range(2 * BMAX + 1)], axis=1
    )
    band_tiles = matrix.reshape(tile_count, TILE, (2 * BMAX + 1) * TILE)
    result = jnp.einsum("uio,uot->uit", band_tiles, windows, precision=lax.Precision.HIGHEST)
    return result.reshape(local_rows, traits_here)


def apply_band(matrix, vector):
    widened = extended_2(vector, (("smp", 0),), TILE * BMAX)
    return band_product(matrix, widened, vector.shape[0], vector.shape[1])


def operate(matrix, seen_mask, vector):
    masked = seen_mask * vector
    return (
        seen_mask * (apply_band(matrix, masked) + ridge_term * masked) + (1.0 - seen_mask) * vector
    )


def squares(residual):
    return lax.psum(jnp.sum(residual * residual, axis=0), "smp")


def local(dosage, allele_mean, snp_scale, band_next, ld_prev, band_prev, zscores, observed):
    band_reach = TILE * BMAX
    local_cols = dosage.shape[1]
    build_tiles = local_cols // TILE
    column_place = lax.axis_index(("snp", "pair"))
    first_col = column_place * local_cols
    mean_here = lax.dynamic_slice_in_dim(allele_mean, first_col, local_cols, 0)
    scale_here = lax.dynamic_slice_in_dim(snp_scale, first_col, local_cols, 0)
    normed = ((dosage.astype(jnp.float32) - mean_here) * scale_here).astype(jnp.bfloat16)
    following = passed_along(normed[:, :band_reach], ("snp", "pair"), -1)
    own_block = transpose_gram(normed, normed)
    cross_part = transpose_gram(normed[:, local_cols - band_reach :], following)
    filler = jnp.zeros((local_cols - band_reach, band_reach), jnp.float32)
    right_window = jnp.concatenate(
        [own_block, jnp.concatenate([filler, cross_part], axis=0)], axis=1
    )
    upper_band = lax.psum(band_of(right_window, TILE, BMAX + 1), "smp")
    upper_tiles = upper_band.reshape(build_tiles, TILE, BMAX + 1, TILE)
    preceding = passed_along(upper_tiles[build_tiles - BMAX :], ("snp", "pair"), 1)
    extended = jnp.concatenate([preceding, upper_tiles], axis=0)
    pieces = []
    for tile_lag in range(BMAX, 0, -1):
        source = extended[BMAX - tile_lag : BMAX - tile_lag + build_tiles, :, tile_lag, :]
        pieces.append(jnp.transpose(source, (0, 2, 1)))
    pieces.append(upper_tiles.reshape(build_tiles, TILE, (BMAX + 1) * TILE))
    gram_band = jnp.concatenate(pieces, axis=2).reshape(local_cols, (2 * BMAX + 1) * TILE)
    samples_total = dosage.shape[0] * lax.axis_size("smp")
    ld_next = local_mask(band_next, column_place, build_tiles) * gram_band / samples_total
    row_place = lax.axis_index("smp")
    local_rows = ld_prev.shape[0]
    solver_tiles = local_rows // TILE
    seen_here = jnp.repeat(observed.astype(jnp.float32), TBLK, axis=1)
    matrix = local_mask(band_prev, row_place, solver_tiles) * ld_prev
    rhs = seen_here * zscores
    solution = jnp.zeros_like(rhs)
    residual = rhs
    direction = rhs
    norm_now = squares(residual)
    for turn_index in range(ITERS):
        image = operate(matrix, seen_here, direction)
        curve = lax.psum(jnp.sum(direction * image, axis=0), "smp")
        step_size = norm_now / curve
        solution = solution + step_size * direction
        residual = residual - step_size * image
        norm_next = squares(residual)
        direction = residual + norm_next / norm_now * direction
        norm_now = norm_next
    imputed = apply_band(matrix, seen_here * solution)
    return (ld_next, imputed)


def solution(mesh):
    return jax.shard_map(
        local,
        mesh=mesh,
        in_specs=(
            P(("grp", "smp"), ("snp", "pair")),
            P("grp"),
            P("grp"),
            P("grp"),
            P(("grp", "smp"), None),
            P("grp"),
            P(("grp", "smp"), ("snp", "pair")),
            P(("grp", "smp"), ("snp", "pair")),
        ),
        out_specs=(P(("grp", "snp", "pair"), None), P(("grp", "smp"), ("snp", "pair"))),
        check_vma=False,
    )
```

profile of v0, /device:TPU:0, one launch (start us, length us, event | category | flops | bytes accessed | tf_op | source)
XLA Modules:
  0.0 323.0 jit_solution(3432829513353105369)
XLA Ops:
  8.6 3.4 %multiply_convert_fusion = bf16[2048,1024]{1,0:T(8,128)(2,1)S(1)} fusion(bf16[2048,1024]{1,0:T(8,128)(2,1)} %param.8, f32[1024]{0:T(1024)S(1)} %dynamic_slice.14, f32[1024]{0:T(1024)S(1)} %dynamic_slice.13), kind=kLoop, calls=%fused_computation.3 | loop fusion | flops 8388608 | bytes 8396800 | tf_op jit(solution)/shard_map/convert_element_type | solution.py:106
  16.1 5.7 %collective-permute-start.2 = (f32[128,128]{0,1:T(8,128)S(1)}, f32[128,128]{0,1:T(8,128)S(1)}, u32[]{:S(2)}, u32[]{:S(2)}) collective-permute-start(f32[128,128]{0,1:T(8,128)S(1)} %get-tuple-element.48), channel_id=1, source_target_pairs={{0,4},{4,8},{8,12},{1,5},{5,9},{9,13},{2,6},{6,10},{10,14},{3,7},{... | collective-permute-start | bytes 196616 | tf_op jit(solution)/shard_map/ppermute | solution.py:23
  21.8 10.0 %fusion.25 = f32[1024,1024]{0,1:T(8,128)} fusion(bf16[2048,1024]{1,0:T(8,128)(2,1)} %copy-done.3), kind=kOutput, calls=%fused_computation.111 | convolution fusion | flops 4294967296 | bytes 8388608 | tf_op jit(solution)/shard_map/dot_general | solution.py:66
  39.2 2.0 copy.59
  42.5 2.0 copy.62
  44.5 1.9 constant_dynamic-update-slice_fusion.3
  49.0 3.7 %fusion.26 = f32[16,64,128]{2,1,0:T(8,128)S(1)} fusion(f32[16,64,320]{2,1,0:T(8,128)S(1)} %bitcast.156, f32[16,320,128]{2,1,0:T(8,128)} %constant_dynamic-update-slice_fusion), kind=kOutput, calls=%fused_computation.112 | convolution fusion | flops 503316480 | bytes 4456448 | tf_op jit(solution)/shard_map/uio,uot->uit/dot_general | solution.py:78
  53.2 10.4 %all-reduce.3 = (f32[128]{0:T(128)S(1)}, f32[128]{0:T(128)S(1)}) all-reduce(f32[128]{0:T(128)S(1)} %get-tuple-element.5, f32[128]{0:T(128)S(1)} %get-tuple-element.4), channel_id=1, replica_groups=mesh['grp'=2,'smp'=4,'snp'=2,'pair'=2] {'smp'}, use_global_device_ids=true, to_apply=%region_2.3 | all-reduce | flops 256 | bytes 2048 | tf_op jit(solution)/shard_map/psum | solution.py:95
  63.9 9.0 %psum.52 = f32[128]{0:T(128)S(1)} all-reduce(f32[128]{0:T(128)S(1)} %multiply_reduce_fusion.2), channel_id=1, replica_groups=mesh['grp'=2,'smp'=4,'snp'=2,'pair'=2] {'smp'}, use_global_device_ids=true, to_apply=%region_6.7 | all-reduce | flops 128 | bytes 1024 | tf_op jit(solution)/shard_map/psum | solution.py:95
  75.3 4.7 %collective-permute-start.4 = (f32[128,128]{0,1:T(8,128)S(1)}, f32[128,128]{0,1:T(8,128)S(1)}, u32[]{:S(2)}, u32[]{:S(2)}) collective-permute-start(f32[128,128]{0,1:T(8,128)S(1)} %get-tuple-element.44), channel_id=1, source_target_pairs={{0,4},{4,8},{8,12},{1,5},{5,9},{9,13},{2,6},{6,10},{10,14},{3,7},{... | collective-permute-start | bytes 196616 | tf_op jit(solution)/shard_map/ppermute | solution.py:23
  80.2 2.0 copy.66
  82.3 3.4 %pad_maximum_fusion.5 = (f32[1024,128]{0,1:T(8,128)}, f32[1024,128]{0,1:T(8,128)}, f32[1024,128]{0,1:T(8,128)}, f32[1024,128]{0,1:T(8,128)}) fusion(f32[128,128]{0,1:T(8,128)S(1)} %collective-permute-done.5, f32[1024,128]{0,1:T(8,128)} %copy-done.2, f32[128,128]{0,1:T(8,128)S(1)} %collective-permute-done.4), kind=kLoop, calls=%fused_computation.55 | loop fusion | flops 524288 | bytes 2752512 | tf_op jit(solution)/shard_map/concatenate | solution.py:21
  85.7 2.0 copy.64
  89.6 2.0 copy.65
  91.6 2.0 copy.67
  93.7 2.1 copy.68
  95.8 1.9 constant_dynamic-update-slice_fusion.8
  102.3 4.5 %fusion.27 = f32[16,64,128]{2,1,0:T(8,128)} fusion(f32[16,64,320]{2,1,0:T(8,128)S(1)} %bitcast.157, f32[16,320,128]{2,1,0:T(8,128)} %constant_dynamic-update-slice_fusion.5), kind=kOutput, calls=%fused_computation.113 | convolution fusion | flops 503316480 | bytes 4456448 | tf_op jit(solution)/shard_map/uio,uot->uit/dot_general | solution.py:78
  106.9 2.1 copy.69
  110.2 10.4 %psum.53 = f32[128]{0:T(128)S(1)} all-reduce(f32[128]{0:T(128)S(1)} %multiply_reduce_fusion.1), channel_id=1, replica_groups=mesh['grp'=2,'smp'=4,'snp'=2,'pair'=2] {'smp'}, use_global_device_ids=true, to_apply=%region_8.9 | all-reduce | flops 128 | bytes 1024 | tf_op jit(solution)/shard_map/psum | solution.py:138
  120.6 2.2 multiply_reduce_fusion
  122.7 8.5 %psum.54 = f32[128]{0:T(128)S(1)} all-reduce(f32[128]{0:T(128)S(1)} %get-tuple-element.8), channel_id=1, replica_groups=mesh['grp'=2,'smp'=4,'snp'=2,'pair'=2] {'smp'}, use_global_device_ids=true, to_apply=%region_10.11 | all-reduce | flops 128 | bytes 1024 | tf_op jit(solution)/shard_map/psum | solution.py:95
  133.7 4.5 %collective-permute-start.6 = (f32[128,128]{0,1:T(8,128)S(1)}, f32[128,128]{0,1:T(8,128)S(1)}, u32[]{:S(2)}, u32[]{:S(2)}) collective-permute-start(f32[128,128]{0,1:T(8,128)S(1)} %get-tuple-element.40), channel_id=1, source_target_pairs={{0,4},{4,8},{8,12},{1,5},{5,9},{9,13},{2,6},{6,10},{10,14},{3,7},{... | collective-permute-start | bytes 196616 | tf_op jit(solution)/shard_map/ppermute | solution.py:23
  141.9 2.0 copy.70
  143.9 2.0 constant_dynamic-update-slice_fusion.14
  145.9 2.0 copy.71
  147.9 2.0 copy.73
  150.0 2.1 copy.74
  152.0 1.9 constant_dynamic-update-slice_fusion.13
  157.6 4.6 %fusion.28 = f32[16,64,128]{2,1,0:T(8,128)} fusion(f32[16,64,320]{2,1,0:T(8,128)S(1)} %bitcast.158, f32[16,320,128]{2,1,0:T(8,128)} %constant_dynamic-update-slice_fusion.10), kind=kOutput, calls=%fused_computation.114 | convolution fusion | flops 503316480 | bytes 4456448 | tf_op jit(solution)/shard_map/uio,uot->uit/dot_general | solution.py:78
  162.2 2.1 copy.75
  165.6 11.4 %psum.55 = f32[128]{0:T(128)S(1)} all-reduce(f32[128]{0:T(128)S(1)} %fusion.16), channel_id=1, replica_groups=mesh['grp'=2,'smp'=4,'snp'=2,'pair'=2] {'smp'}, use_global_device_ids=true, to_apply=%region_12.13 | all-reduce | flops 128 | bytes 1024 | tf_op jit(solution)/shard_map/psum | solution.py:138
  178.1 2.1 copy.78
  182.9 4.8 %collective-permute-start.8 = (f32[128,128]{0,1:T(8,128)S(1)}, f32[128,128]{0,1:T(8,128)S(1)}, u32[]{:S(2)}, u32[]{:S(2)}) collective-permute-start(f32[128,128]{0,1:T(8,128)S(1)} %get-tuple-element.36), channel_id=1, source_target_pairs={{0,4},{4,8},{8,12},{1,5},{5,9},{9,13},{2,6},{6,10},{10,14},{3,7},{... | collective-permute-start | bytes 196616 | tf_op jit(solution)/shard_map/ppermute | solution.py:23
  189.3 5.1 %select_maximum_fusion = f32[1024,1152]{0,1:T(8,128)} fusion(f32[128,128]{0,1:T(8,128)S(1)} %fusion.18, f32[1024,1024]{0,1:T(8,128)} %fusion.25), kind=kLoop, calls=%fused_computation.4 | loop fusion | flops 3538944 | bytes 8978432 | tf_op jit(solution)/shard_map/concatenate | solution.py:111
  194.4 8.2 %reshape.85 = f32[16,64,18,64]{1,0,3,2:T(8,128)} reshape(f32[1024,1152]{0,1:T(8,128)} %select_maximum_fusion) | data formatting | bytes 9437184 | tf_op jit(solution)/shard_map/reshape | solution.py:41
  202.5 17.3 %fusion.20 = (f32[16,64,16,64]{1,0,3,2:T(8,128)}, f32[16,64,16,64]{1,0,3,2:T(8,128)}, f32[16,64,16,64]{1,0,3,2:T(8,128)}) fusion(f32[16,64,18,64]{1,0,3,2:T(8,128)} %reshape.85), kind=kLoop, calls=%fused_computation.106 | loop fusion | bytes 25165824 | tf_op jit(solution)/shard_map/slice | solution.py:44
  219.8 8.7 %copy.83 = f32[16,64,16,64]{3,1,2,0:T(8,128)} copy(f32[16,64,16,64]{1,0,3,2:T(8,128)} %get-tuple-element.14) | data formatting | bytes 8388608
  228.5 8.7 %copy.82 = f32[16,64,16,64]{3,1,2,0:T(8,128)} copy(f32[16,64,16,64]{1,0,3,2:T(8,128)} %get-tuple-element.13) | data formatting | bytes 8388608
  237.2 4.0 %gather_fusion.2 = f32[16,64,64]{2,1,0:T(8,128)S(1)} fusion(f32[64,64,16,16]{1,0,3,2:T(8,128)} %bitcast.160, s32[16]{0:T(128)S(1)} %or_bitcast_fusion), kind=kCustom, calls=%fused_computation.2 | custom fusion | bytes 524416 | tf_op jit(solution)/shard_map/jit(diagonal)/gather | solution.py:44
  241.2 4.0 %gather_fusion.1 = f32[16,64,64]{2,1,0:T(8,128)S(1)} fusion(f32[64,64,16,16]{1,0,3,2:T(8,128)} %bitcast.161, s32[16]{0:T(128)S(1)} %or_bitcast_fusion), kind=kCustom, calls=%fused_computation.1 | custom fusion | bytes 524416 | tf_op jit(solution)/shard_map/jit(diagonal)/gather | solution.py:44
  245.1 8.7 %copy.81 = f32[16,64,16,64]{3,1,2,0:T(8,128)} copy(f32[16,64,16,64]{1,0,3,2:T(8,128)} %get-tuple-element.12) | data formatting | bytes 8388608
  253.8 4.0 %gather_fusion = f32[16,64,64]{2,1,0:T(8,128)S(1)} fusion(f32[64,64,16,16]{1,0,3,2:T(8,128)} %bitcast.162, s32[16]{0:T(128)S(1)} %or_bitcast_fusion), kind=kCustom, calls=%fused_computation | custom fusion | bytes 524416 | tf_op jit(solution)/shard_map/jit(diagonal)/gather | solution.py:44
  259.1 2.5 copy.53
  263.0 2.0 copy.76
  273.8 30.6 %all-reduce.6.cloned.1.call-done = f32[1024,192]{0,1:T(8,128)} async-done(((f32[1024,192]{0,1:T(8,128)}), f32[1024,192]{0,1:T(8,128)}) %all-reduce.6.cloned.1.call-update) | async-done | bytes 786448 | tf_op jit(solution)/shard_map/psum | solution.py:114
  305.5 2.3 collective-permute-start.1
  307.8 4.6 %fusion.29 = f32[16,64,128]{2,1,0:T(8,128)} fusion(f32[16,64,320]{2,1,0:T(8,128)S(1)} %bitcast.159, f32[16,320,128]{2,1,0:T(8,128)} %constant_dynamic-update-slice_fusion.15), kind=kOutput, calls=%fused_computation.115 | convolution fusion | flops 503316480 | bytes 4456448 | tf_op jit(solution)/shard_map/uio,uot->uit/dot_general | solution.py:78
  (121 shorter events, 60.3 us)
Async XLA Ops:
  7.2 297.2 %all-reduce.6.cloned.1.call-start = ((), (), s32[]{:S(2)}) async-start(), calls=%async_computation | async-start | bytes 1572864 | tf_op jit(solution)/shard_map/psum | solution.py:114
  8.6 5.8 %copy-start.12 = (s32[1024,2]{0,1:T(2,128)S(1)}, s32[1024,2]{0,1:T(2,128)}, u32[]{:S(2)}) copy-start(s32[1024,2]{0,1:T(2,128)} %param.15) | copy-start | bytes 24580
  8.6 5.8 %copy-start.11 = (f32[1024,128]{1,0:T(8,128)S(1)}, f32[1024,128]{1,0:T(8,128)}, u32[]{:S(2)}) copy-start(f32[1024,128]{1,0:T(8,128)} %param.14) | copy-start | bytes 1572868
  12.0 2.4 copy-start.3
  13.1 174.6 %collective-permute-start = (bf16[2048,128]{1,0:T(8,128)(2,1)}, bf16[2048,128]{1,0:T(8,128)(2,1)}, u32[]{:S(2)}, u32[]{:S(2)}) collective-permute-start(bf16[2048,128]{1,0:T(8,128)(2,1)} %slice.273), channel_id=1, source_target_pairs={{1,0},{2,1},{3,2},{5,4},{6,5},{7,6},{9,8},{10,9},{11,10},{13,12},{... | collective-permute-start | bytes 1572872 | tf_op jit(solution)/shard_map/ppermute | solution.py:35
  14.7 20.6 %collective-permute-start.3 = (f32[128,128]{0,1:T(8,128)S(1)}, f32[128,128]{0,1:T(8,128)S(1)}, u32[]{:S(2)}, u32[]{:S(2)}) collective-permute-start(f32[128,128]{0,1:T(8,128)S(1)} %get-tuple-element.47), channel_id=1, source_target_pairs={{4,0},{8,4},{12,8},{5,1},{9,5},{13,9},{6,2},{10,6},{14,10},{7,3},{... | collective-permute-start | bytes 196616 | tf_op jit(solution)/shard_map/ppermute | solution.py:25
  16.0 15.9 %copy-start.13 = (s32[64]{0:T(128)S(1)}, s32[64]{0:T(128)}, u32[]{:S(2)}) copy-start(s32[64]{0:T(128)} %param.13) | copy-start | bytes 772
  16.1 15.9 %copy-start.14 = (s32[64]{0:T(128)S(1)}, s32[64]{0:T(128)}, u32[]{:S(2)}) copy-start(s32[64]{0:T(128)} %param.11) | copy-start | bytes 772
  16.1 16.3 %copy-start.10 = (f32[1024,320]{0,1:T(8,128)S(1)}, f32[1024,320]{0,1:T(8,128)}, u32[]{:S(2)}) copy-start(f32[1024,320]{0,1:T(8,128)} %param.12) | copy-start | bytes 3932164
  16.1 19.3 %collective-permute-start.2 = (f32[128,128]{0,1:T(8,128)S(1)}, f32[128,128]{0,1:T(8,128)S(1)}, u32[]{:S(2)}, u32[]{:S(2)}) collective-permute-start(f32[128,128]{0,1:T(8,128)S(1)} %get-tuple-element.48), channel_id=1, source_target_pairs={{0,4},{4,8},{8,12},{1,5},{5,9},{9,13},{2,6},{6,10},{10,14},{3,7},{... | collective-permute-start | bytes 196616 | tf_op jit(solution)/shard_map/ppermute | solution.py:23
  44.5 3.6 %copy-start.7 = (f32[1024,128]{1,0:T(8,128)S(1)}, f32[1024,128]{1,0:T(8,128)}, u32[]{:S(2)}) copy-start(f32[1024,128]{1,0:T(8,128)} %copy.62) | copy-start | bytes 1572868
  73.1 0.8 copy-start.2
  74.0 8.3 %collective-permute-start.5 = (f32[128,128]{0,1:T(8,128)S(1)}, f32[128,128]{0,1:T(8,128)S(1)}, u32[]{:S(2)}, u32[]{:S(2)}) collective-permute-start(f32[128,128]{0,1:T(8,128)S(1)} %get-tuple-element.43), channel_id=1, source_target_pairs={{4,0},{8,4},{12,8},{5,1},{9,5},{13,9},{6,2},{10,6},{14,10},{7,3},{... | collective-permute-start | bytes 196616 | tf_op jit(solution)/shard_map/ppermute | solution.py:25
  75.3 7.0 %collective-permute-start.4 = (f32[128,128]{0,1:T(8,128)S(1)}, f32[128,128]{0,1:T(8,128)S(1)}, u32[]{:S(2)}, u32[]{:S(2)}) collective-permute-start(f32[128,128]{0,1:T(8,128)S(1)} %get-tuple-element.44), channel_id=1, source_target_pairs={{0,4},{4,8},{8,12},{1,5},{5,9},{9,13},{2,6},{6,10},{10,14},{3,7},{... | collective-permute-start | bytes 196616 | tf_op jit(solution)/shard_map/ppermute | solution.py:23
  95.8 5.7 %copy-start.8 = (f32[1024,128]{1,0:T(8,128)S(1)}, f32[1024,128]{1,0:T(8,128)}, u32[]{:S(2)}) copy-start(f32[1024,128]{1,0:T(8,128)} %copy.68) | copy-start | bytes 1572868
  132.4 6.9 %collective-permute-start.7 = (f32[128,128]{0,1:T(8,128)S(1)}, f32[128,128]{0,1:T(8,128)S(1)}, u32[]{:S(2)}, u32[]{:S(2)}) collective-permute-start(f32[128,128]{0,1:T(8,128)S(1)} %get-tuple-element.39), channel_id=1, source_target_pairs={{4,0},{8,4},{12,8},{5,1},{9,5},{13,9},{6,2},{10,6},{14,10},{7,3},{... | collective-permute-start | bytes 196616 | tf_op jit(solution)/shard_map/ppermute | solution.py:25
  133.7 6.4 %collective-permute-start.6 = (f32[128,128]{0,1:T(8,128)S(1)}, f32[128,128]{0,1:T(8,128)S(1)}, u32[]{:S(2)}, u32[]{:S(2)}) collective-permute-start(f32[128,128]{0,1:T(8,128)S(1)} %get-tuple-element.40), channel_id=1, source_target_pairs={{0,4},{4,8},{8,12},{1,5},{5,9},{9,13},{2,6},{6,10},{10,14},{3,7},{... | collective-permute-start | bytes 196616 | tf_op jit(solution)/shard_map/ppermute | solution.py:23
  143.9 10.1 %copy-start.6 = (f32[1024,128]{1,0:T(8,128)S(1)}, f32[1024,128]{1,0:T(8,128)}, u32[]{:S(2)}) copy-start(f32[1024,128]{1,0:T(8,128)} %copy.72) | copy-start | bytes 1572868
  152.0 4.7 %copy-start.9 = (f32[1024,128]{1,0:T(8,128)S(1)}, f32[1024,128]{1,0:T(8,128)}, u32[]{:S(2)}) copy-start(f32[1024,128]{1,0:T(8,128)} %copy.74) | copy-start | bytes 1572868
  157.6 6.7 %copy-start = (f32[1024,128]{0,1:T(8,128)S(1)}, f32[1024,128]{0,1:T(8,128)}, u32[]{:S(2)}) copy-start(f32[1024,128]{0,1:T(8,128)} %get-tuple-element.9) | copy-start | bytes 1572868
  181.6 80.0 %collective-permute-start.9 = (f32[128,128]{0,1:T(8,128)}, f32[128,128]{0,1:T(8,128)S(1)}, u32[]{:S(2)}, u32[]{:S(2)}) collective-permute-start(f32[128,128]{0,1:T(8,128)} %get-tuple-element.35), channel_id=1, source_target_pairs={{4,0},{8,4},{12,8},{5,1},{9,5},{13,9},{6,2},{10,6},{14,10},{7,3},{... | collective-permute-start | bytes 196616 | tf_op jit(solution)/shard_map/ppermute | solution.py:25
  182.9 78.7 %collective-permute-start.8 = (f32[128,128]{0,1:T(8,128)S(1)}, f32[128,128]{0,1:T(8,128)S(1)}, u32[]{:S(2)}, u32[]{:S(2)}) collective-permute-start(f32[128,128]{0,1:T(8,128)S(1)} %get-tuple-element.36), channel_id=1, source_target_pairs={{0,4},{4,8},{8,12},{1,5},{5,9},{9,13},{2,6},{6,10},{10,14},{3,7},{... | collective-permute-start | bytes 196616 | tf_op jit(solution)/shard_map/ppermute | solution.py:23
  259.1 2.5 copy-start.1
  265.0 6.2 %copy-start.5 = (f32[1024,128]{1,0:T(8,128)S(1)}, f32[1024,128]{1,0:T(8,128)}, u32[]{:S(2)}) copy-start(f32[1024,128]{1,0:T(8,128)} %copy.78) | copy-start | bytes 1572868
  304.3 8.0 %copy-start.4 = (f32[1024,192]{0,1:T(8,128)S(1)}, f32[1024,192]{0,1:T(8,128)}, u32[]{:S(2)}) copy-start(f32[1024,192]{0,1:T(8,128)} %all-reduce.6.cloned.1.call-done) | copy-start | bytes 2359300
  305.5 7.3 %collective-permute-start.1 = (f32[2,64,3,64]{1,0,3,2:T(2,128)S(1)}, f32[2,64,3,64]{1,0,3,2:T(2,128)}, u32[]{:S(2)}, u32[]{:S(2)}) collective-permute-start(f32[2,64,3,64]{1,0,3,2:T(2,128)S(1)} %slice.215), channel_id=1, source_target_pairs={{0,1},{1,2},{2,3},{4,5},{5,6},{6,7},{8,9},{9,10},{10,11},{12,13},{... | collective-permute-start | bytes 294920 | tf_op jit(solution)/shard_map/ppermute | solution.py:35
Sparse Core Ops, SparseCore 0:
  261.8 42.5 all-reduce.5
where the time goes:
time: 327 us; the launch traced here: 323 us
  local copies, waits for them, and re-layouts  140 us (43%)
  blocking collectives  49.7 us (15%)
  waiting for transfers between devices  31.5 us (10%)
  other arithmetic  29.4 us (9%)
  matrix products  29 us (9%)
  starting transfers between devices  28.5 us (9%)
  between operations  14.5 us (4%)
    unnamed x50, local copies, waits for them, and re-layouts  51.3 us
    psum x1, waiting for transfers between devices, local(): upper_band = lax.psum(band_of(right_window, TILE, BMAX + 1), 'smp')  30.6 us
    psum x3, blocking collectives, squares(): return lax.psum(jnp.sum(residual * residual, axis=0), 'smp')  27.9 us
    slice x16, local copies, waits for them, and re-layouts, band_product(): stacked[offset:offset + tile_count]  27.4 us
    psum x2, blocking collectives, local(): curve = lax.psum(jnp.sum(direction * image, axis=0), 'smp')  21.8 us
    ppermute x4, starting transfers between devices, extended_2(): lax.ppermute(tail, axis, [(i, (i + 1) % count) for i in range(ends)])  19.7 us
    dot_general x4, matrix products, band_product(): jnp.einsum('uio,uot->uit', band_tiles, windows, precision=lax.Precision.H...  17.4 us
    slice x1, local copies, waits for them, and re-layouts, band_of(): blocks[:, :, offset:offset + tile_count, :]  17.3 us
  transfers between devices with their start and end apart: 11, of which 2 were waited for; matrix products, arithmetic and copies ran while one was open for 58% of the time, Pallas kernels for 0%

commit v1 on v0

v1 whole, which is shorter than its diff:
```python
import functools
import jax
import jax.numpy as jnp
from jax import lax
from jax.sharding import PartitionSpec as P
from jax.experimental import pallas as pl
from jax.experimental.pallas import tpu as pltpu

TILE = 64
BMAX = 2
TBLK = 64
SPAN = 2 * BMAX + 1
REACH = TILE * BMAX
PAIR = 2 * TILE
LANES = 128
WIDE = 384
CHUNK = 256
STEP = 64
F32 = jnp.float32
BF16 = jnp.bfloat16
MESH = pl.DeviceIdType.MESH

ridge_term = 1.0


def split_two(value):
    high = value.astype(BF16)
    low = (value - high.astype(F32)).astype(BF16)
    return high, low


def folded(value):
    return jnp.sum(value.reshape(value.shape[0] // 8, 8, value.shape[1]), axis=0)


def total_row(value):
    return jnp.sum(value, axis=0, keepdims=True)


def tile_flags(widths, tile, count):
    here = widths[tile]
    flags = []
    for offset in range(-BMAX, BMAX + 1):
        place = tile + offset
        inside = (place >= 0) & (place < count)
        beside = widths[jnp.clip(place, 0, count - 1)]
        reach = abs(offset)
        flags.append(jnp.where(inside & (here >= reach) & (beside >= reach), 1.0, 0.0).astype(F32))
    return flags


def mask_row(flags, rows, width):
    lane_tile = lax.broadcasted_iota(jnp.int32, (rows, width), 1) // TILE
    mask = jnp.zeros((rows, width), F32)
    for index, flag in enumerate(flags):
        mask = jnp.where(lane_tile == index, flag, mask)
    return mask


def kernel(
    sizes,
    dosage, mean, scale, band_next, ld_prev, band_prev, zscores, seen,
    ld_next, imputed,
    dos, dos_side, normed, gram, moving, edge_in, edge_out,
    vec, vec_two, band_two, image, res1, img0, red,
    dos_sem, side_sem, vec_send, vec_recv, red_send, red_recv, mov_send, mov_recv, edge_sem,
):
    n_smp, n_snp, n_pair = sizes
    samples, cols = dos.shape
    rows = zscores.shape[0]
    tiles = rows // TILE
    chunks = cols // CHUNK
    blocks = cols // PAIR
    tile_total = band_next.shape[0]
    me = lax.axis_index("smp")
    place = lax.axis_index("snp") * n_pair + lax.axis_index("pair")
    places = n_snp * n_pair
    first_col = place * cols
    order = list(range(1, chunks)) + [0]

    def at_place(index):
        return {"snp": index // n_pair, "pair": index % n_pair}

    has_left, has_right = place > 0, place < places - 1
    has_prev, has_next = me > 0, me < n_smp - 1
    left_id = at_place(jnp.maximum(place - 1, 0))
    right_id = at_place(jnp.minimum(place + 1, places - 1))

    fetches = []
    for chunk in order:
        span = pl.ds(chunk * CHUNK, CHUNK)
        fetch = pltpu.make_async_copy(dosage.at[:, span], dos.at[:, span], dos_sem.at[chunk])
        fetch.start()
        fetches.append(fetch)

    barrier = pltpu.get_barrier_semaphore()
    for step in range(1, n_smp):
        pl.semaphore_signal(
            barrier, inc=1, device_id={"smp": lax.rem(me + step, n_smp)}, device_id_type=MESH
        )

    @pl.when(has_left)
    def _():
        pl.semaphore_signal(barrier, inc=1, device_id=left_id, device_id_type=MESH)

    @pl.when(has_right)
    def _():
        pl.semaphore_signal(barrier, inc=1, device_id=right_id, device_id_type=MESH)

    tail = vec_two.shape[1] - REACH - rows
    for turn in range(3):
        vec_two[turn, pl.ds(REACH + rows, tail), :] = jnp.zeros((tail, 2 * LANES), BF16)

        @pl.when(me == 0)
        def _():
            vec[turn, pl.ds(0, REACH), :] = jnp.zeros((REACH, LANES), F32)

        @pl.when(me == n_smp - 1)
        def _():
            vec[turn, pl.ds(REACH + rows, REACH), :] = jnp.zeros((REACH, LANES), F32)

    def put_vector(turn, tile, value):
        span = pl.ds(pl.multiple_of(REACH + tile * TILE, TILE), TILE)
        vec[turn, span, :] = value
        high, low = split_two(value)
        vec_two[turn, span, 0:LANES] = high
        vec_two[turn, span, LANES : 2 * LANES] = low

    def own_rows(tile):
        return pl.ds(pl.multiple_of(tile * TILE, TILE), TILE)

    def vec_rows(tile):
        return pl.ds(pl.multiple_of(REACH + tile * TILE, TILE), TILE)

    def first_vector(tile, carry):
        put_vector(0, tile, seen[own_rows(tile), :] * zscores[own_rows(tile), :])
        return carry

    lax.fori_loop(0, tiles, first_vector, 0)

    pl.semaphore_wait(
        barrier,
        n_smp - 1 + jnp.where(has_left, 1, 0) + jnp.where(has_right, 1, 0),
    )

    side_copy = pltpu.make_async_remote_copy(
        src_ref=dosage.at[:, pl.ds(0, REACH)],
        dst_ref=dos_side,
        send_sem=side_sem.at[0],
        recv_sem=side_sem.at[1],
        device_id=left_id,
        device_id_type=MESH,
    )

    def halo_copies(turn):
        up = pltpu.make_async_remote_copy(
            src_ref=vec.at[turn, pl.ds(REACH, REACH)],
            dst_ref=vec.at[turn, pl.ds(REACH + rows, REACH)],
            send_sem=vec_send.at[turn, 0],
            recv_sem=vec_recv.at[turn, 0],
            device_id={"smp": jnp.maximum(me - 1, 0)},
            device_id_type=MESH,
        )
        down = pltpu.make_async_remote_copy(
            src_ref=vec.at[turn, pl.ds(rows, REACH)],
            dst_ref=vec.at[turn, pl.ds(0, REACH)],
            send_sem=vec_send.at[turn, 1],
            recv_sem=vec_recv.at[turn, 1],
            device_id={"smp": jnp.minimum(me + 1, n_smp - 1)},
            device_id_type=MESH,
        )
        return up, down

    def send_halos(turn):
        up, down = halo_copies(turn)

        @pl.when(has_prev)
        def _():
            up.start()

        @pl.when(has_next)
        def _():
            down.start()

    def take_halos(turn):
        up, down = halo_copies(turn)

        @pl.when(has_next)
        def _():
            up.wait_recv()

        @pl.when(has_prev)
        def _():
            down.wait_recv()

        for start in (0, REACH + rows):
            high, low = split_two(vec[turn, pl.ds(start, REACH), :])
            vec_two[turn, pl.ds(start, REACH), 0:LANES] = high
            vec_two[turn, pl.ds(start, REACH), LANES : 2 * LANES] = low

    def red_copy(turn, step):
        return pltpu.make_async_remote_copy(
            src_ref=red.at[turn, me],
            dst_ref=red.at[turn, me],
            send_sem=red_send.at[turn, step],
            recv_sem=red_recv.at[turn, step],
            device_id={"smp": lax.rem(me + step, n_smp)},
            device_id_type=MESH,
        )

    def red_arrival(turn, step):
        sender = lax.rem(me - step + n_smp, n_smp)
        return pltpu.make_async_remote_copy(
            src_ref=red.at[turn, sender],
            dst_ref=red.at[turn, sender],
            send_sem=red_send.at[turn, step],
            recv_sem=red_recv.at[turn, step],
            device_id={"smp": lax.rem(me + step, n_smp)},
            device_id_type=MESH,
        )

    def send_sums(turn, sums):
        lines = [total_row(value) for value in sums]
        lines += [jnp.zeros((1, LANES), F32)] * (8 - len(lines))
        red[turn, me] = jnp.concatenate(lines, axis=0)
        for step in range(1, n_smp):
            red_copy(turn, step).start()

    def take_sums(turn):
        for step in range(1, n_smp):
            red_arrival(turn, step).wait_recv()
        whole = red[turn, 0]
        for index in range(1, n_smp):
            whole = whole + red[turn, index]
        return whole

    @pl.when(has_left)
    def _():
        side_copy.start()

    send_halos(0)

    def band_tile(tile, carry):
        flags = tile_flags(band_prev, me * tiles + tile, tile_total)
        here = ld_prev[own_rows(tile), :] * mask_row(flags, TILE, SPAN * TILE)
        here = jnp.concatenate([here, jnp.zeros((TILE, WIDE - SPAN * TILE), F32)], axis=1)
        high, low = split_two(here)
        band_two[tile, 0:TILE, :] = high
        band_two[tile, TILE : 2 * TILE, :] = low
        return carry

    lax.fori_loop(0, tiles, band_tile, 0)

    def normalise(source, source_col, width, global_col, target_col):
        where = pl.ds(pl.multiple_of(global_col, LANES), width)
        mean_part = mean[:, where]
        scale_part = scale[:, where]

        def body(index, carry):
            span = pl.ds(pl.multiple_of(index * STEP, STEP), STEP)
            value = source[span, source_col : source_col + width].astype(F32)
            normed[span, target_col : target_col + width] = (
                (value - mean_part) * scale_part
            ).astype(BF16)
            return carry

        lax.fori_loop(0, samples // STEP, body, 0)

    ready = set()

    def make_ready(chunk):
        if chunk in ready:
            return
        ready.add(chunk)
        if chunk < chunks:
            fetches[order.index(chunk)].wait()
            normalise(dos, chunk * CHUNK, CHUNK, first_col + chunk * CHUNK, chunk * CHUNK)
            return

        @pl.when(has_right)
        def _():
            side_copy.wait_recv()
            normalise(dos_side, 0, REACH, first_col + cols, cols)

        @pl.when(jnp.logical_not(has_right))
        def _():
            normed[:, cols : cols + REACH] = jnp.zeros((samples, REACH), BF16)

    def make_gram(chunk):
        make_ready(chunk)
        make_ready(chunk + 1)
        low = chunk * CHUNK
        own = normed[:, low : low + CHUNK]
        window = normed[:, low : low + CHUNK + REACH]
        part = lax.dot_general(own, window, (((0,), (0,)), ((), ())), preferred_element_type=F32)
        gram[2 * chunk] = part[0:PAIR, 0 : 2 * PAIR]
        gram[2 * chunk + 1] = part[PAIR : 2 * PAIR, PAIR : 3 * PAIR]

    half = n_smp // 2
    first_way = jnp.where(me < half, 0, 1)
    second_way = 1 - first_way
    at_end = (me == 0) | (me == n_smp - 1)

    def running_copy(way, chunk):
        return pltpu.make_async_remote_copy(
            src_ref=moving.at[way, pl.ds(2 * chunk, 2)],
            dst_ref=moving.at[way, pl.ds(2 * chunk, 2)],
            send_sem=mov_send.at[way, chunk],
            recv_sem=mov_recv.at[way, chunk],
            device_id={"smp": jnp.clip(me + 1 - 2 * way, 0, n_smp - 1)},
            device_id_type=MESH,
        )

    def first_pass_end(chunk):
        @pl.when(at_end)
        def _():
            moving[first_way, pl.ds(2 * chunk, 2)] = gram[pl.ds(2 * chunk, 2)]
            running_copy(first_way, chunk).start()

    def first_pass_inner(chunk):
        @pl.when(jnp.logical_not(at_end))
        def _():
            running_copy(first_way, chunk).wait_recv()
            moving[first_way, pl.ds(2 * chunk, 2)] += gram[pl.ds(2 * chunk, 2)]
            running_copy(first_way, chunk).start()

    def edge_copy():
        return pltpu.make_async_remote_copy(
            src_ref=edge_out,
            dst_ref=edge_in,
            send_sem=edge_sem.at[0],
            recv_sem=edge_sem.at[1],
            device_id=right_id,
            device_id_type=MESH,
        )

    def second_pass(chunk):
        span = pl.ds(2 * chunk, 2)
        running_copy(second_way, chunk).wait_recv()
        other = moving[second_way, span]
        summed = moving[first_way, span] + other

        @pl.when(jnp.logical_not(at_end))
        def _():
            moving[second_way, span] = other + gram[span]
            running_copy(second_way, chunk).start()

        gram[span] = summed
        if chunk == chunks - 1:
            edge_out[...] = gram[blocks - 1, :, PAIR : 2 * PAIR]

            @pl.when(has_right)
            def _():
                edge_copy().start()

    def product(turn, tile):
        window = vec_two[turn, pl.ds(pl.multiple_of(tile * TILE, TILE), WIDE), :]
        out = jnp.dot(band_two[tile], window, preferred_element_type=F32)
        value = (out[0:TILE, 0:LANES] + out[TILE:, LANES:]) + (
            out[0:TILE, LANES:] + out[TILE:, 0:LANES]
        )
        image[turn, own_rows(tile), :] = value
        return value

    def operated(turn, tile, vector):
        flag = seen[own_rows(tile), :]
        masked = flag * vector
        return flag * (product(turn, tile) + ridge_term * masked) + (1.0 - flag) * vector

    def over_tiles(turn, body, start):
        inner = max(tiles - 2 * BMAX, 0)
        edges = list(range(min(BMAX, tiles))) + list(range(max(tiles - BMAX, BMAX), tiles))
        carry = start
        if inner:
            unroll = 4 if inner % 4 == 0 else 1
            carry = lax.fori_loop(BMAX, BMAX + inner, body, carry, unroll=unroll)
        take_halos(turn)
        for tile in edges:
            carry = body(tile, carry)
        return carry

    nothing = jnp.zeros((8, LANES), F32)

    def start_solver():
        def body(tile, carry):
            square, cross = carry
            here = vec[0, vec_rows(tile), :]
            out = operated(0, tile, here)
            put_vector(1, tile, seen[own_rows(tile), :] * out)
            return square + folded(here * here), cross + folded(here * out)

        square, cross = over_tiles(0, body, (nothing, nothing))
        send_halos(1)
        send_sums(0, [square, cross])

    def next_solver():
        def body(tile, carry):
            img0[own_rows(tile), :] = operated(1, tile, vec[1, vec_rows(tile), :])
            return carry

        over_tiles(1, body, 0)
        whole = take_sums(0)
        norm0, curve0 = whole[0:1], whole[1:2]
        alpha0 = norm0 / curve0

        def update(tile, carry):
            square, cross, mixed = carry
            r0 = vec[0, vec_rows(tile), :]
            w0 = vec[1, vec_rows(tile), :]
            r1 = r0 - alpha0 * w0
            w1 = w0 - alpha0 * img0[own_rows(tile), :]
            res1[own_rows(tile), :] = r1
            put_vector(2, tile, seen[own_rows(tile), :] * w1)
            return (
                square + folded(r1 * r1),
                cross + folded(r1 * w1),
                mixed + folded(r1 * w0 + r0 * w1),
            )

        sums = lax.fori_loop(0, tiles, update, (nothing, nothing, nothing), unroll=2)
        send_halos(2)
        send_sums(1, list(sums))
        return norm0, curve0, alpha0

    def last_solver(norm0, curve0, alpha0):
        def body(tile, carry):
            here = vec[2, vec_rows(tile), :]
            imputed[own_rows(tile), :] = operated(2, tile, here)
            return carry

        over_tiles(2, body, 0)
        whole = take_sums(1)
        norm1 = whole[0:1]
        beta1 = norm1 / norm0
        curve1 = whole[1:2] + beta1 * whole[2:3] + beta1 * beta1 * curve0
        alpha1 = norm1 / curve1

        def update(tile, carry):
            square, cross, mixed = carry
            r0 = vec[0, vec_rows(tile), :]
            w0 = vec[1, vec_rows(tile), :]
            r1 = res1[own_rows(tile), :]
            w1 = vec[2, vec_rows(tile), :]
            p1 = r1 + beta1 * r0
            s1 = w1 + beta1 * w0
            z1 = imputed[own_rows(tile), :] + beta1 * img0[own_rows(tile), :]
            r2 = r1 - alpha1 * s1
            w2 = w1 - alpha1 * z1
            return (
                square + folded(r2 * r2),
                cross + folded(r2 * w2),
                mixed + folded(r2 * s1 + p1 * w2),
            )

        sums = lax.fori_loop(0, tiles, update, (nothing, nothing, nothing), unroll=2)
        send_sums(2, list(sums))
        return norm1, curve1, alpha1, beta1

    def end_solver(alpha0, norm1, curve1, alpha1, beta1):
        whole = take_sums(2)
        beta2 = whole[0:1] / norm1
        curve2 = whole[1:2] + beta2 * whole[2:3] + beta2 * beta2 * curve1
        alpha2 = whole[0:1] / curve2
        first = (1.0 + beta1, -alpha0)
        second = (
            1.0 + beta2 * first[0],
            -alpha0 - alpha1 * beta1 + beta2 * first[1],
            -alpha1,
        )
        part0 = alpha0 + alpha1 * first[0] + alpha2 * second[0]
        part1 = alpha1 * first[1] + alpha2 * second[1]
        part2 = alpha2 * second[2]

        def body(tile, carry):
            span = own_rows(tile)
            imputed[span, :] = (
                part0 * image[0, span, :] + part1 * image[1, span, :] + part2 * image[2, span, :]
            )
            return carry

        lax.fori_loop(0, tiles, body, 0, unroll=2)

    middle = (chunks + 1) // 2
    for chunk in order[:middle]:
        make_gram(chunk)
        first_pass_end(chunk)
    start_solver()
    for chunk in order[middle:]:
        make_gram(chunk)
        first_pass_end(chunk)
    scalars0 = next_solver()
    for chunk in order:
        first_pass_inner(chunk)
    scalars1 = last_solver(*scalars0)
    for chunk in order[:middle]:
        second_pass(chunk)
    end_solver(scalars0[2], *scalars1)
    for chunk in order[middle:]:
        second_pass(chunk)

    inverse = 1.0 / (samples * n_smp)

    def assemble(block, before):
        turned = jnp.transpose(before)
        tile = 2 * block
        whole = jnp.concatenate([turned, gram[block]], axis=1)
        for side in range(2):
            flags = tile_flags(band_next, place * (cols // TILE) + tile + side, tile_total)
            flags = [flag * inverse for flag in flags]
            part = whole[side * TILE : (side + 1) * TILE]
            if side:
                part = pltpu.roll(part, WIDE - TILE, 1)
            part = part * mask_row(flags, TILE, WIDE)
            ld_next[pl.ds((tile + side) * TILE, TILE), :] = part[:, 0 : SPAN * TILE]

    for block in range(1, blocks):
        assemble(block, gram[block - 1, :, PAIR : 2 * PAIR])

    @pl.when(has_left)
    def _():
        edge_copy().wait_recv()

    @pl.when(jnp.logical_not(has_left))
    def _():
        edge_in[...] = jnp.zeros((PAIR, PAIR), F32)

    assemble(0, edge_in[...])

    @pl.when(has_left)
    def _():
        side_copy.wait_send()

    @pl.when(has_right)
    def _():
        edge_copy().wait_send()

    for turn in range(3):
        up, down = halo_copies(turn)

        @pl.when(has_prev)
        def _():
            up.wait_send()

        @pl.when(has_next)
        def _():
            down.wait_send()

        for step in range(1, n_smp):
            red_copy(turn, step).wait_send()

    for chunk in range(chunks):
        running_copy(first_way, chunk).wait_send()

        @pl.when(jnp.logical_not(at_end))
        def _():
            running_copy(second_way, chunk).wait_send()


def local(sizes, dosage, allele_mean, snp_scale, band_next, ld_prev, band_prev, zscores, observed):
    n_smp = sizes[0]
    samples, cols = dosage.shape
    rows, traits = zscores.shape
    tiles = rows // TILE
    chunks, blocks = cols // CHUNK, cols // PAIR
    seen = jnp.repeat(observed.astype(F32), TBLK, axis=1)
    if traits < LANES:
        seen = jnp.pad(seen, ((0, 0), (0, LANES - traits)))
        zscores = jnp.pad(zscores, ((0, 0), (0, LANES - traits)))
    vmem = pl.BlockSpec(memory_space=pltpu.VMEM)
    smem = pl.BlockSpec(memory_space=pltpu.SMEM)
    dma = pltpu.SemaphoreType.DMA
    ld_next, imputed = pl.pallas_call(
        functools.partial(kernel, sizes),
        out_shape=(
            jax.ShapeDtypeStruct((cols, SPAN * TILE), F32),
            jax.ShapeDtypeStruct((rows, LANES), F32),
        ),
        in_specs=[
            pl.BlockSpec(memory_space=pl.ANY), vmem, vmem, smem, vmem, smem, vmem, vmem,
        ],
        out_specs=(vmem, vmem),
        scratch_shapes=[
            pltpu.VMEM((samples, cols), BF16),
            pltpu.VMEM((samples, REACH), BF16),
            pltpu.VMEM((samples, cols + REACH), BF16),
            pltpu.VMEM((blocks, PAIR, 2 * PAIR), F32),
            pltpu.VMEM((2, blocks, PAIR, 2 * PAIR), F32),
            pltpu.VMEM((PAIR, PAIR), F32),
            pltpu.VMEM((PAIR, PAIR), F32),
            pltpu.VMEM((3, rows + 2 * REACH, LANES), F32),
            pltpu.VMEM((3, rows + 2 * REACH + WIDE - SPAN * TILE, 2 * LANES), BF16),
            pltpu.VMEM((tiles, 2 * TILE, WIDE), BF16),
            pltpu.VMEM((3, rows, LANES), F32),
            pltpu.VMEM((rows, LANES), F32),
            pltpu.VMEM((rows, LANES), F32),
            pltpu.VMEM((3, n_smp, 8, LANES), F32),
            dma((chunks,)),
            dma((2,)),
            dma((3, 2)),
            dma((3, 2)),
            dma((3, n_smp)),
            dma((3, n_smp)),
            dma((2, chunks)),
            dma((2, chunks)),
            dma((2,)),
        ],
        compiler_params=pltpu.CompilerParams(
            collective_id=0, has_side_effects=True, vmem_limit_bytes=48 * 1024 * 1024
        ),
    )(
        dosage,
        allele_mean.reshape(1, -1),
        snp_scale.reshape(1, -1),
        band_next,
        ld_prev,
        band_prev,
        zscores,
        seen,
    )
    return ld_next, imputed[:, :traits]


def solution(mesh):
    sizes = (mesh.shape["smp"], mesh.shape["snp"], mesh.shape["pair"])
    return jax.shard_map(
        functools.partial(local, sizes),
        mesh=mesh,
        in_specs=(
            P(("grp", "smp"), ("snp", "pair")),
            P("grp"),
            P("grp"),
            P("grp"),
            P(("grp", "smp"), None),
            P("grp"),
            P(("grp", "smp"), ("snp", "pair")),
            P(("grp", "smp"), ("snp", "pair")),
        ),
        out_specs=(P(("grp", "snp", "pair"), None), P(("grp", "smp"), ("snp", "pair"))),
        check_vma=False,
    )
```

time: 327 us -> 70.6 us (0.22); the launches traced: 323 us -> 70.4 us
  local copies, waits for them, and re-layouts: 140 us -> 6.95 us
  Pallas kernels: 0 us -> 62 us
  blocking collectives: 49.7 us -> 0 us
  waiting for transfers between devices: 31.5 us -> 0 us
  matrix products: 29 us -> 0 us
  other arithmetic: 29.4 us -> 0.7 us
  starting transfers between devices: 28.5 us -> 0 us
  between operations: 14.5 us -> 0.75 us
    pallas_call x0 -> x1, Pallas kernels: none -> 62 us  [local(): pl.pallas_call(functools.partial(kernel, sizes), out_shape=(jax.ShapeDtyp...]
    psum x5 -> x0, blocking collectives: 49.7 us -> none  [the longest x3 27.9 us: squares(): return lax.psum(jnp.sum(residual * residual, axis=0), 'smp')]
    slice x24 -> x0, local copies, waits for them, and re-layouts: 48.4 us -> none  [the longest x16 27.4 us: band_product(): stacked[offset:offset + tile_count]]
    unnamed x50 -> x14, local copies, waits for them, and re-layouts: 51.3 us -> 3.8 us
    psum x1 -> x0, waiting for transfers between devices: 30.6 us -> none  [local(): upper_band = lax.psum(band_of(right_window, TILE, BMAX + 1), 'smp')]
    dot_general x6 -> x0, matrix products: 29 us -> none  [the longest x4 17.4 us: band_product(): jnp.einsum('uio,uot->uit', band_tiles, windows, precision=lax.Precision.H...]
    ppermute x10 -> x0, starting transfers between devices: 28.5 us -> none  [the longest x4 19.7 us: extended_2(): lax.ppermute(tail, axis, [(i, (i + 1) % count) for i in range(ends)])]
    reshape x8 -> x1, local copies, waits for them, and re-layouts: 15.6 us -> 0.19 us  [local(): seen = jnp.repeat(observed.astype(F32), TBLK, axis=1)]
  transfers between devices with their start and end apart: 11 -> 0, of which waited for: 2 -> 0; matrix products, arithmetic and copies ran while one was open for 58% -> 0% of each run, Pallas kernels for 0% -> 0%
where the time goes in v1:
time: 70.6 us; the launch traced here: 70.4 us
  Pallas kernels  62 us (88%)
  local copies, waits for them, and re-layouts  6.95 us (10%)
  between operations  0.75 us (1%)
    pallas_call x1, Pallas kernels, local(): pl.pallas_call(functools.partial(kernel, sizes), out_shape=(jax.ShapeDtyp...  62 us
    unnamed x14, local copies, waits for them, and re-layouts  3.8 us
    pallas_call x1, local copies, waits for them, and re-layouts, local(): pl.pallas_call(functools.partial(kernel, sizes), out_shape=(jax.ShapeDtyp...  2.92 us

profile of v1, /device:TPU:0, one launch (start us, length us, event | category | flops | bytes accessed | tf_op | source)
XLA Modules:
  0.0 70.4 jit_solution(8522375608754956879)
XLA Ops:
  0.6 0.7 convert_element_type.3
  1.4 0.2 copy.14.seen
  1.6 0.0 copy-start.1
  1.6 0.0 copy-start.2
  1.6 0.0 copy-start.3
  1.6 0.0 copy-start.4
  1.6 0.0 copy-start.5
  1.6 1.8 %copy.13.ld_prev = f32[1024,320]{1,0:T(8,128)S(1)} copy(f32[1024,320]{0,1:T(8,128)} %param.12) | data formatting | bytes 2621440 | tf_op args[4]
  3.5 0.0 copy-done.1
  3.5 0.0 copy-done.2
  3.5 0.0 copy-done.3
  3.5 0.0 copy-done.4
  3.5 0.0 copy-done.5
  3.5 62.0 %shard_map.95 = (f32[1024,320]{1,0:T(8,128)S(1)}, f32[1024,128]{1,0:T(8,128)S(1)}) custom-call(bf16[2048,1024]{1,0:T(8,128)(2,1)} %dosage.1, f32[1,4096]{1,0:T(1,128)S(1)} %bitcast.3, f32[1,4096]{1,0:T(1,128)S(1)} %bitcast.4, s32[64]{0:T(128)S(1)} %copy-done.4, f32[1024,320]{1,0:T(8,128)S(1)} %copy.13.ld_prev, s32[64]{0:T(128)S(1)} %copy-done.5, ...), custom_call_target="tpu_custom_call" | custom-call | tf_op jit(solution)/shard_map/pallas_call | solution.py:572
  65.5 0.0 copy-start
  65.5 1.1 %copy-done = f32[1024,320]{1,0:T(8,128)} copy-done((f32[1024,320]{1,0:T(8,128)}, f32[1024,320]{1,0:T(8,128)S(1)}, u32[]{:S(2)}) %copy-start) | copy-done | bytes 1310744
  66.7 2.9 %copy.15 = f32[1024,320]{0,1:T(8,128)} copy(f32[1024,320]{1,0:T(8,128)} %copy-done) | data formatting | bytes 2621440 | tf_op jit(solution)/shard_map/pallas_call | solution.py:572
  69.6 0.8 %copy.17 = f32[1024,128]{1,0:T(8,128)} copy(f32[1024,128]{1,0:T(8,128)S(1)} %get-tuple-element.9) | data formatting | bytes 1048576
  (1 shorter events, 0.0 us)
Async XLA Ops:
  1.6 1.9 %copy-start.1 = (f32[1024,128]{1,0:T(8,128)S(1)}, f32[1024,128]{1,0:T(8,128)}, u32[]{:S(2)}) copy-start(f32[1024,128]{1,0:T(8,128)} %zscores.1) | copy-start | bytes 1572868
  1.6 1.9 %copy-start.2 = (f32[4096]{0:T(1024)S(1)}, f32[4096]{0:T(1024)}, u32[]{:S(2)}) copy-start(f32[4096]{0:T(1024)} %param.9) | copy-start | bytes 49156
  1.6 1.9 %copy-start.3 = (f32[4096]{0:T(1024)S(1)}, f32[4096]{0:T(1024)}, u32[]{:S(2)}) copy-start(f32[4096]{0:T(1024)} %param.10) | copy-start | bytes 49156
  1.6 1.9 %copy-start.4 = (s32[64]{0:T(128)S(1)}, s32[64]{0:T(128)}, u32[]{:S(2)}) copy-start(s32[64]{0:T(128)} %band_next.1) | copy-start | bytes 772
  1.6 1.9 %copy-start.5 = (s32[64]{0:T(128)S(1)}, s32[64]{0:T(128)}, u32[]{:S(2)}) copy-start(s32[64]{0:T(128)} %band_prev.1) | copy-start | bytes 772
  65.5 1.2 %copy-start = (f32[1024,320]{1,0:T(8,128)}, f32[1024,320]{1,0:T(8,128)S(1)}, u32[]{:S(2)}) copy-start(f32[1024,320]{1,0:T(8,128)S(1)} %get-tuple-element.4) | copy-start | bytes 3932164

commit v2 on v1

--- a/solution.py
+++ b/solution.py
@@ -15,7 +15,9 @@
 LANES = 128
 WIDE = 384
 CHUNK = 256
-STEP = 64
+STEP = 128
+CODE_TOP = 32767.0
+CODE_LEAST = 1e-30
 F32 = jnp.float32
 BF16 = jnp.bfloat16
 MESH = pl.DeviceIdType.MESH
@@ -49,21 +51,15 @@
     return flags
 
 
-def mask_row(flags, rows, width):
-    lane_tile = lax.broadcasted_iota(jnp.int32, (rows, width), 1) // TILE
-    mask = jnp.zeros((rows, width), F32)
-    for index, flag in enumerate(flags):
-        mask = jnp.where(lane_tile == index, flag, mask)
-    return mask
-
-
 def kernel(
     sizes,
-    dosage, mean, scale, band_next, ld_prev, band_prev, zscores, seen,
+    dosage, mean, scale, band_next, ld_hbm, band_prev, z_hbm, observed,
     ld_next, imputed,
-    dos, dos_side, normed, gram, moving, edge_in, edge_out,
+    ld_prev, zscores, seen,
+    dos, dos_side, normed, gram, summed, code_out, code_in, peak_out, peak_in, edge_in,
     vec, vec_two, band_two, image, res1, img0, red,
-    dos_sem, side_sem, vec_send, vec_recv, red_send, red_recv, mov_send, mov_recv, edge_sem,
+    in_sem, dos_sem, side_sem, vec_send, vec_recv, red_send, red_recv,
+    code_send, code_recv, peak_send, peak_recv, edge_sem,
 ):
     n_smp, n_snp, n_pair = sizes
     samples, cols = dos.shape
@@ -71,6 +67,7 @@
     tiles = rows // TILE
     chunks = cols // CHUNK
     blocks = cols // PAIR
+    row_blocks = rows // PAIR
     tile_total = band_next.shape[0]
     me = lax.axis_index("smp")
     place = lax.axis_index("snp") * n_pair + lax.axis_index("pair")
@@ -86,6 +83,10 @@
     left_id = at_place(jnp.maximum(place - 1, 0))
     right_id = at_place(jnp.minimum(place + 1, places - 1))
 
+    z_fetch = pltpu.make_async_copy(z_hbm, zscores, in_sem.at[0])
+    ld_fetch = pltpu.make_async_copy(ld_hbm, ld_prev, in_sem.at[1])
+    z_fetch.start()
+    ld_fetch.start()
     fetches = []
     for chunk in order:
         span = pl.ds(chunk * CHUNK, CHUNK)
@@ -106,42 +107,6 @@
     @pl.when(has_right)
     def _():
         pl.semaphore_signal(barrier, inc=1, device_id=right_id, device_id_type=MESH)
-
-    tail = vec_two.shape[1] - REACH - rows
-    for turn in range(3):
-        vec_two[turn, pl.ds(REACH + rows, tail), :] = jnp.zeros((tail, 2 * LANES), BF16)
-
-        @pl.when(me == 0)
-        def _():
-            vec[turn, pl.ds(0, REACH), :] = jnp.zeros((REACH, LANES), F32)
-
-        @pl.when(me == n_smp - 1)
-        def _():
-            vec[turn, pl.ds(REACH + rows, REACH), :] = jnp.zeros((REACH, LANES), F32)
-
-    def put_vector(turn, tile, value):
-        span = pl.ds(pl.multiple_of(REACH + tile * TILE, TILE), TILE)
-        vec[turn, span, :] = value
-        high, low = split_two(value)
-        vec_two[turn, span, 0:LANES] = high
-        vec_two[turn, span, LANES : 2 * LANES] = low
-
-    def own_rows(tile):
-        return pl.ds(pl.multiple_of(tile * TILE, TILE), TILE)
-
-    def vec_rows(tile):
-        return pl.ds(pl.multiple_of(REACH + tile * TILE, TILE), TILE)
-
-    def first_vector(tile, carry):
-        put_vector(0, tile, seen[own_rows(tile), :] * zscores[own_rows(tile), :])
-        return carry
-
-    lax.fori_loop(0, tiles, first_vector, 0)
-
-    pl.semaphore_wait(
-        barrier,
-        n_smp - 1 + jnp.where(has_left, 1, 0) + jnp.where(has_right, 1, 0),
-    )
 
     side_copy = pltpu.make_async_remote_copy(
         src_ref=dosage.at[:, pl.ds(0, REACH)],
@@ -151,6 +116,38 @@
         device_id=left_id,
         device_id_type=MESH,
     )
+
+    for turn in range(3):
+
+        @pl.when(me == 0)
+        def _():
+            vec[turn, pl.ds(0, REACH), :] = jnp.zeros((REACH, LANES), F32)
+
+        @pl.when(me == n_smp - 1)
+        def _():
+            vec[turn, pl.ds(REACH + rows, REACH), :] = jnp.zeros((REACH, LANES), F32)
+
+    pl.semaphore_wait(
+        barrier,
+        n_smp - 1 + jnp.where(has_left, 1, 0) + jnp.where(has_right, 1, 0),
+    )
+
+    @pl.when(has_left)
+    def _():
+        side_copy.start()
+
+    def put_vector(turn, tile, value):
+        span = pl.ds(pl.multiple_of(REACH + tile * PAIR, PAIR), PAIR)
+        vec[turn, span, :] = value
+        high, low = split_two(value)
+        vec_two[turn, span, 0:LANES] = high
+        vec_two[turn, span, LANES : 2 * LANES] = low
+
+    def own_rows(tile):
+        return pl.ds(pl.multiple_of(tile * PAIR, PAIR), PAIR)
+
+    def vec_rows(tile):
+        return pl.ds(pl.multiple_of(REACH + tile * PAIR, PAIR), PAIR)
 
     def halo_copies(turn):
         up = pltpu.make_async_remote_copy(
@@ -234,22 +231,45 @@
             whole = whole + red[turn, index]
         return whole
 
-    @pl.when(has_left)
-    def _():
-        side_copy.start()
+    lane = lax.broadcasted_iota(jnp.int32, (PAIR, LANES), 1)
+    line = lax.broadcasted_iota(jnp.int32, (PAIR, LANES), 0)
+
+    z_fetch.wait()
+    for tile in range(row_blocks):
+        here = observed[:, pl.ds(tile * PAIR, PAIR)].astype(F32)
+        flags = jnp.zeros((LANES, PAIR), F32)
+        for index in range(here.shape[0]):
+            flags = jnp.where(line // TBLK == index, here[index : index + 1], flags)
+        flags = jnp.transpose(flags)
+        seen[pl.ds(tile * PAIR, PAIR), :] = flags
+        put_vector(0, tile, flags * zscores[pl.ds(tile * PAIR, PAIR), :])
 
     send_halos(0)
 
-    def band_tile(tile, carry):
-        flags = tile_flags(band_prev, me * tiles + tile, tile_total)
-        here = ld_prev[own_rows(tile), :] * mask_row(flags, TILE, SPAN * TILE)
-        here = jnp.concatenate([here, jnp.zeros((TILE, WIDE - SPAN * TILE), F32)], axis=1)
-        high, low = split_two(here)
-        band_two[tile, 0:TILE, :] = high
-        band_two[tile, TILE : 2 * TILE, :] = low
-        return carry
-
-    lax.fori_loop(0, tiles, band_tile, 0)
+    ld_fetch.wait()
+
+    def two_flags(widths, first_tile, factor):
+        left = tile_flags(widths, first_tile, tile_total)
+        right = tile_flags(widths, first_tile + 1, tile_total)
+        first_lanes = lane[0:1] < TILE
+        return [jnp.where(first_lanes, a * factor, b * factor) for a, b in zip(left, right)]
+
+    for tile in range(row_blocks):
+        flags = two_flags(band_prev, me * tiles + 2 * tile, 1.0)
+        columns = pl.ds(tile * PAIR, PAIR)
+        parts = [
+            ld_prev[pl.ds(index * TILE, TILE), columns] * flag for index, flag in enumerate(flags)
+        ]
+        blank = jnp.zeros((TILE, PAIR), F32)
+        left, right = parts + [blank], [blank] + parts
+        for third in range(3):
+            pieces = [
+                jnp.where(lane[0:TILE] < TILE, left[index], right[index])
+                for index in (2 * third, 2 * third + 1)
+            ]
+            high, low = split_two(jnp.transpose(jnp.concatenate(pieces, axis=0)))
+            band_two[tile, 0:PAIR, third * PAIR : (third + 1) * PAIR] = high
+            band_two[tile, PAIR : 2 * PAIR, third * PAIR : (third + 1) * PAIR] = low
 
     def normalise(source, source_col, width, global_col, target_col):
         where = pl.ds(pl.multiple_of(global_col, LANES), width)
@@ -293,40 +313,80 @@
         own = normed[:, low : low + CHUNK]
         window = normed[:, low : low + CHUNK + REACH]
         part = lax.dot_general(own, window, (((0,), (0,)), ((), ())), preferred_element_type=F32)
-        gram[2 * chunk] = part[0:PAIR, 0 : 2 * PAIR]
-        gram[2 * chunk + 1] = part[PAIR : 2 * PAIR, PAIR : 3 * PAIR]
+        first, second = part[0:PAIR, 0:PAIR], part[PAIR:, PAIR : 2 * PAIR]
+        gram[chunk, 0] = jnp.where(line <= lane, first, second)
+        spare = total_row(jnp.where(line == lane, second, 0.0))
+        unused = (line < TILE) & (lane >= TILE)
+        for side in range(2):
+            beside = part[side * PAIR : (side + 1) * PAIR, (side + 1) * PAIR : (side + 2) * PAIR]
+            held = spare if side == 0 else pltpu.roll(spare, TILE, 1)
+            held = jnp.where(line == 0, held, 0.0)
+            gram[chunk, 1 + side] = jnp.where(unused, held, beside)
 
     half = n_smp // 2
     first_way = jnp.where(me < half, 0, 1)
     second_way = 1 - first_way
     at_end = (me == 0) | (me == n_smp - 1)
 
-    def running_copy(way, chunk):
-        return pltpu.make_async_remote_copy(
-            src_ref=moving.at[way, pl.ds(2 * chunk, 2)],
-            dst_ref=moving.at[way, pl.ds(2 * chunk, 2)],
-            send_sem=mov_send.at[way, chunk],
-            recv_sem=mov_recv.at[way, chunk],
-            device_id={"smp": jnp.clip(me + 1 - 2 * way, 0, n_smp - 1)},
-            device_id_type=MESH,
-        )
+    def running_copies(way, chunk):
+        ahead = {"smp": jnp.clip(me + 1 - 2 * way, 0, n_smp - 1)}
+        return [
+            pltpu.make_async_remote_copy(
+                src_ref=source.at[way, chunk],
+                dst_ref=target.at[way, chunk],
+                send_sem=send.at[way, chunk],
+                recv_sem=recv.at[way, chunk],
+                device_id=ahead,
+                device_id_type=MESH,
+            )
+            for source, target, send, recv in (
+                (code_out, code_in, code_send, code_recv),
+                (peak_out, peak_in, peak_send, peak_recv),
+            )
+        ]
+
+    def send_running(way, chunk, values):
+        peaks = []
+        for index, value in enumerate(values):
+            peak = jnp.max(jnp.abs(value), axis=0, keepdims=True)
+            factor = CODE_TOP / jnp.maximum(peak, CODE_LEAST)
+            code = jnp.round(value * factor).astype(jnp.int32)
+            code_out[way, chunk, index] = code.astype(jnp.int16)
+            peaks.append(peak)
+        peaks += [jnp.zeros((1, LANES), F32)] * (8 - len(peaks))
+        peak_out[way, chunk] = jnp.concatenate(peaks, axis=0)
+        for copy in running_copies(way, chunk):
+            copy.start()
+
+    def take_running(way, chunk):
+        for copy in running_copies(way, chunk):
+            copy.wait_recv()
+        peaks = peak_in[way, chunk] * (1.0 / CODE_TOP)
+        return [
+            code_in[way, chunk, index].astype(jnp.int32).astype(F32) * peaks[index : index + 1]
+            for index in range(3)
+        ]
 
     def first_pass_end(chunk):
         @pl.when(at_end)
         def _():
-            moving[first_way, pl.ds(2 * chunk, 2)] = gram[pl.ds(2 * chunk, 2)]
-            running_copy(first_way, chunk).start()
+            values = [gram[chunk, index] for index in range(3)]
+            for index in range(3):
+                summed[chunk, index] = values[index]
+            send_running(first_way, chunk, values)
 
     def first_pass_inner(chunk):
         @pl.when(jnp.logical_not(at_end))
         def _():
-            running_copy(first_way, chunk).wait_recv()
-            moving[first_way, pl.ds(2 * chunk, 2)] += gram[pl.ds(2 * chunk, 2)]
-            running_copy(first_way, chunk).start()
+            values = take_running(first_way, chunk)
+            values = [value + gram[chunk, index] for index, value in enumerate(values)]
+            for index in range(3):
+                summed[chunk, index] = values[index]
+            send_running(first_way, chunk, values)
 
     def edge_copy():
         return pltpu.make_async_remote_copy(
-            src_ref=edge_out,
+            src_ref=summed.at[chunks - 1, 2],
             dst_ref=edge_in,
             send_sem=edge_sem.at[0],
             recv_sem=edge_sem.at[1],
@@ -335,29 +395,29 @@
         )
 
     def second_pass(chunk):
-        span = pl.ds(2 * chunk, 2)
-        running_copy(second_way, chunk).wait_recv()
-        other = moving[second_way, span]
-        summed = moving[first_way, span] + other
+        values = take_running(second_way, chunk)
 
         @pl.when(jnp.logical_not(at_end))
         def _():
-            moving[second_way, span] = other + gram[span]
-            running_copy(second_way, chunk).start()
-
-        gram[span] = summed
+            send_running(
+                second_way,
+                chunk,
+                [value + gram[chunk, index] for index, value in enumerate(values)],
+            )
+
+        for index in range(3):
+            summed[chunk, index] += values[index]
         if chunk == chunks - 1:
-            edge_out[...] = gram[blocks - 1, :, PAIR : 2 * PAIR]
 
             @pl.when(has_right)
             def _():
                 edge_copy().start()
 
     def product(turn, tile):
-        window = vec_two[turn, pl.ds(pl.multiple_of(tile * TILE, TILE), WIDE), :]
+        window = vec_two[turn, pl.ds(pl.multiple_of(tile * PAIR, PAIR), WIDE), :]
         out = jnp.dot(band_two[tile], window, preferred_element_type=F32)
-        value = (out[0:TILE, 0:LANES] + out[TILE:, LANES:]) + (
-            out[0:TILE, LANES:] + out[TILE:, 0:LANES]
+        value = (out[0:PAIR, 0:LANES] + out[PAIR:, LANES:]) + (
+            out[0:PAIR, LANES:] + out[PAIR:, 0:LANES]
         )
         image[turn, own_rows(tile), :] = value
         return value
@@ -368,12 +428,12 @@
         return flag * (product(turn, tile) + ridge_term * masked) + (1.0 - flag) * vector
 
     def over_tiles(turn, body, start):
-        inner = max(tiles - 2 * BMAX, 0)
-        edges = list(range(min(BMAX, tiles))) + list(range(max(tiles - BMAX, BMAX), tiles))
+        inner = max(row_blocks - 2, 0)
+        edges = sorted({0, row_blocks - 1})
         carry = start
         if inner:
-            unroll = 4 if inner % 4 == 0 else 1
-            carry = lax.fori_loop(BMAX, BMAX + inner, body, carry, unroll=unroll)
+            unroll = 2 if inner % 2 == 0 else 1
+            carry = lax.fori_loop(1, 1 + inner, body, carry, unroll=unroll)
         take_halos(turn)
         for tile in edges:
             carry = body(tile, carry)
@@ -417,7 +477,7 @@
                 mixed + folded(r1 * w0 + r0 * w1),
             )
 
-        sums = lax.fori_loop(0, tiles, update, (nothing, nothing, nothing), unroll=2)
+        sums = lax.fori_loop(0, row_blocks, update, (nothing, nothing, nothing))
         send_halos(2)
         send_sums(1, list(sums))
         return norm0, curve0, alpha0
@@ -452,7 +512,7 @@
                 mixed + folded(r2 * s1 + p1 * w2),
             )
 
-        sums = lax.fori_loop(0, tiles, update, (nothing, nothing, nothing), unroll=2)
+        sums = lax.fori_loop(0, row_blocks, update, (nothing, nothing, nothing))
         send_sums(2, list(sums))
         return norm1, curve1, alpha1, beta1
 
@@ -478,7 +538,7 @@
             )
             return carry
 
-        lax.fori_loop(0, tiles, body, 0, unroll=2)
+        lax.fori_loop(0, row_blocks, body, 0)
 
     middle = (chunks + 1) // 2
     for chunk in order[:middle]:
@@ -495,26 +555,47 @@
     for chunk in order[:middle]:
         second_pass(chunk)
     end_solver(scalars0[2], *scalars1)
+
+    inverse = 1.0 / (samples * n_smp)
+
+    def assemble(block, before):
+        chunk, side = block // 2, block % 2
+        packed = summed[chunk, 0]
+        turned = jnp.transpose(packed)
+        if side:
+            spare = jnp.where(
+                lane[0:1] >= TILE,
+                summed[chunk, 1, 0:1],
+                pltpu.roll(summed[chunk, 2, 0:1], TILE, 1),
+            )
+            diagonal = jnp.where(line > lane, packed, jnp.where(line < lane, turned, spare))
+        else:
+            diagonal = jnp.where(line <= lane, packed, turned)
+        after = jnp.transpose(summed[chunk, 1 + side])
+        stack = [before[0:TILE], before[TILE:], diagonal[0:TILE], diagonal[TILE:]]
+        stack += [after[0:TILE], after[TILE:]]
+        flags = two_flags(band_next, place * (cols // TILE) + 2 * block, inverse)
+        for index, flag in enumerate(flags):
+            value = jnp.where(lane[0:TILE] < TILE, stack[index], stack[index + 1])
+            ld_next[pl.ds(index * TILE, TILE), pl.ds(block * PAIR, PAIR)] = value * flag
+
+    done = set()
+
+    def assemble_ready():
+        for block in range(1, blocks):
+            needed = {block // 2, (block - 1) // 2}
+            if block not in assembled and needed <= done:
+                assembled.add(block)
+                assemble(block, summed[(block - 1) // 2, 1 + (block - 1) % 2])
+
+    assembled = set()
+    for chunk in order[:middle]:
+        done.add(chunk)
+    assemble_ready()
     for chunk in order[middle:]:
         second_pass(chunk)
-
-    inverse = 1.0 / (samples * n_smp)
-
-    def assemble(block, before):
-        turned = jnp.transpose(before)
-        tile = 2 * block
-        whole = jnp.concatenate([turned, gram[block]], axis=1)
-        for side in range(2):
-            flags = tile_flags(band_next, place * (cols // TILE) + tile + side, tile_total)
-            flags = [flag * inverse for flag in flags]
-            part = whole[side * TILE : (side + 1) * TILE]
-            if side:
-                part = pltpu.roll(part, WIDE - TILE, 1)
-            part = part * mask_row(flags, TILE, WIDE)
-            ld_next[pl.ds((tile + side) * TILE, TILE), :] = part[:, 0 : SPAN * TILE]
-
-    for block in range(1, blocks):
-        assemble(block, gram[block - 1, :, PAIR : 2 * PAIR])
+        done.add(chunk)
+        assemble_ready()
 
     @pl.when(has_left)
     def _():
@@ -549,57 +630,66 @@
             red_copy(turn, step).wait_send()
 
     for chunk in range(chunks):
-        running_copy(first_way, chunk).wait_send()
+        for copy in running_copies(first_way, chunk):
+            copy.wait_send()
 
         @pl.when(jnp.logical_not(at_end))
         def _():
-            running_copy(second_way, chunk).wait_send()
+            for copy in running_copies(second_way, chunk):
+                copy.wait_send()
 
 
 def local(sizes, dosage, allele_mean, snp_scale, band_next, ld_prev, band_prev, zscores, observed):
     n_smp = sizes[0]
     samples, cols = dosage.shape
     rows, traits = zscores.shape
-    tiles = rows // TILE
-    chunks, blocks = cols // CHUNK, cols // PAIR
-    seen = jnp.repeat(observed.astype(F32), TBLK, axis=1)
+    chunks = cols // CHUNK
     if traits < LANES:
-        seen = jnp.pad(seen, ((0, 0), (0, LANES - traits)))
         zscores = jnp.pad(zscores, ((0, 0), (0, LANES - traits)))
     vmem = pl.BlockSpec(memory_space=pltpu.VMEM)
+    far = pl.BlockSpec(memory_space=pl.ANY)
     smem = pl.BlockSpec(memory_space=pltpu.SMEM)
     dma = pltpu.SemaphoreType.DMA
     ld_next, imputed = pl.pallas_call(
         functools.partial(kernel, sizes),
         out_shape=(
-            jax.ShapeDtypeStruct((cols, SPAN * TILE), F32),
+            jax.ShapeDtypeStruct((SPAN * TILE, cols), F32),
             jax.ShapeDtypeStruct((rows, LANES), F32),
         ),
         in_specs=[
-            pl.BlockSpec(memory_space=pl.ANY), vmem, vmem, smem, vmem, smem, vmem, vmem,
+            far, vmem, vmem, smem, far, smem, far, vmem,
         ],
         out_specs=(vmem, vmem),
         scratch_shapes=[
+            pltpu.VMEM((SPAN * TILE, rows), F32),
+            pltpu.VMEM((rows, LANES), F32),
+            pltpu.VMEM((rows, LANES), F32),
             pltpu.VMEM((samples, cols), BF16),
             pltpu.VMEM((samples, REACH), BF16),
             pltpu.VMEM((samples, cols + REACH), BF16),
-            pltpu.VMEM((blocks, PAIR, 2 * PAIR), F32),
-            pltpu.VMEM((2, blocks, PAIR, 2 * PAIR), F32),
-            pltpu.VMEM((PAIR, PAIR), F32),
+            pltpu.VMEM((chunks, 3, PAIR, PAIR), F32),
+            pltpu.VMEM((chunks, 3, PAIR, PAIR), F32),
+            pltpu.VMEM((2, chunks, 3, PAIR, PAIR), jnp.int16),
+            pltpu.VMEM((2, chunks, 3, PAIR, PAIR), jnp.int16),
+            pltpu.VMEM((2, chunks, 8, PAIR), F32),
+            pltpu.VMEM((2, chunks, 8, PAIR), F32),
             pltpu.VMEM((PAIR, PAIR), F32),
             pltpu.VMEM((3, rows + 2 * REACH, LANES), F32),
-            pltpu.VMEM((3, rows + 2 * REACH + WIDE - SPAN * TILE, 2 * LANES), BF16),
-            pltpu.VMEM((tiles, 2 * TILE, WIDE), BF16),
+            pltpu.VMEM((3, rows + 2 * REACH, 2 * LANES), BF16),
+            pltpu.VMEM((rows // PAIR, 2 * PAIR, WIDE), BF16),
             pltpu.VMEM((3, rows, LANES), F32),
             pltpu.VMEM((rows, LANES), F32),
             pltpu.VMEM((rows, LANES), F32),
             pltpu.VMEM((3, n_smp, 8, LANES), F32),
+            dma((2,)),
             dma((chunks,)),
             dma((2,)),
             dma((3, 2)),
             dma((3, 2)),
             dma((3, n_smp)),
             dma((3, n_smp)),
+            dma((2, chunks)),
+            dma((2, chunks)),
             dma((2, chunks)),
             dma((2, chunks)),
             dma((2,)),
@@ -612,12 +702,12 @@
         allele_mean.reshape(1, -1),
         snp_scale.reshape(1, -1),
         band_next,
-        ld_prev,
+        jnp.transpose(ld_prev),
         band_prev,
         zscores,
-        seen,
+        jnp.transpose(observed),
     )
-    return ld_next, imputed[:, :traits]
+    return jnp.transpose(ld_next), imputed[:, :traits]
 
 
 def solution(mesh):

time: 70.6 us -> 46 us (0.65)
  Pallas kernels: 62 us -> 37.3 us
    pallas_call x1, Pallas kernels: 62 us -> 37.3 us  [local(): pl.pallas_call(functools.partial(kernel, sizes), out_shape=(jax.ShapeDtyp...]
    unnamed x14 -> x16, local copies, waits for them, and re-layouts: 3.8 us -> 7.64 us
    pallas_call x1 -> x0, local copies, waits for them, and re-layouts: 2.92 us -> none  [local(): pl.pallas_call(functools.partial(kernel, sizes), out_shape=(jax.ShapeDtyp...]
where the time goes in v2:
time: 46 us; the launch traced here: 45.6 us
  Pallas kernels  37.3 us (81%)
  local copies, waits for them, and re-layouts  7.64 us (17%)
  between operations  0.66 us (1%)
    pallas_call x1, Pallas kernels, local(): pl.pallas_call(functools.partial(kernel, sizes), out_shape=(jax.ShapeDtyp...  37.3 us
    unnamed x16, local copies, waits for them, and re-layouts  7.64 us

profile of v2, /device:TPU:0, one launch (start us, length us, event | category | flops | bytes accessed | tf_op | source)
XLA Modules:
  0.0 45.6 jit_solution(2635854189272061780)
XLA Ops:
  0.6 0.0 copy-start
  0.6 1.3 %copy-done = f32[1024,320]{0,1:T(8,128)S(1)} copy-done((f32[1024,320]{0,1:T(8,128)S(1)}, f32[1024,320]{0,1:T(8,128)}, u32[]{:S(2)}) %copy-start) | copy-done | bytes 1310744
  1.9 0.0 copy-start.1
  2.0 1.0 %copy-done.1 = f32[1024,128]{1,0:T(8,128)S(1)} copy-done((f32[1024,128]{1,0:T(8,128)S(1)}, f32[1024,128]{1,0:T(8,128)}, u32[]{:S(2)}) %copy-start.1) | copy-done | bytes 524312
  3.0 0.0 copy-start.2
  3.0 0.7 %copy-done.2 = f32[4096]{0:T(1024)S(1)} copy-done((f32[4096]{0:T(1024)S(1)}, f32[4096]{0:T(1024)}, u32[]{:S(2)}) %copy-start.2) | copy-done | bytes 16408
  3.7 0.0 copy-start.3
  3.7 0.7 %copy-done.3 = f32[4096]{0:T(1024)S(1)} copy-done((f32[4096]{0:T(1024)S(1)}, f32[4096]{0:T(1024)}, u32[]{:S(2)}) %copy-start.3) | copy-done | bytes 16408
  4.4 0.0 copy-start.4
  4.4 0.7 %copy-done.4 = s32[1024,2]{0,1:T(2,128)S(1)} copy-done((s32[1024,2]{0,1:T(2,128)S(1)}, s32[1024,2]{0,1:T(2,128)}, u32[]{:S(2)}) %copy-start.4) | copy-done | bytes 8216
  5.1 0.0 copy-start.5
  5.1 0.7 %copy-done.5 = s32[64]{0:T(128)S(1)} copy-done((s32[64]{0:T(128)S(1)}, s32[64]{0:T(128)}, u32[]{:S(2)}) %copy-start.5) | copy-done | bytes 280
  5.8 0.0 copy-start.6
  5.8 0.7 %copy-done.6 = s32[64]{0:T(128)S(1)} copy-done((s32[64]{0:T(128)S(1)}, s32[64]{0:T(128)}, u32[]{:S(2)}) %copy-start.6) | copy-done | bytes 280
  6.4 37.3 %shard_map.95 = (f32[320,1024]{1,0:T(8,128)S(1)}, f32[1024,128]{1,0:T(8,128)S(1)}) custom-call(bf16[2048,1024]{1,0:T(8,128)(2,1)} %dosage.1, f32[1,4096]{1,0:T(1,128)S(1)} %bitcast.7, f32[1,4096]{1,0:T(1,128)S(1)} %bitcast.8, s32[64]{0:T(128)S(1)} %copy-done.5, f32[320,1024]{1,0:T(8,128)S(1)} %bitcast.5, s32[64]{0:T(128)S(1)} %copy-done.6, ...), custom_call_target="tpu_custom_call" | custom-call | tf_op jit(solution)/shard_map/pallas_call | solution.py:653
  43.7 1.1 %copy.12 = f32[1024,320]{0,1:T(8,128)} copy(f32[1024,320]{0,1:T(8,128)S(1)} %bitcast.6) | data formatting | bytes 2621440
  44.8 0.8 %copy.13 = f32[1024,128]{1,0:T(8,128)} copy(f32[1024,128]{1,0:T(8,128)S(1)} %get-tuple-element.9) | data formatting | bytes 1048576
Async XLA Ops:
  0.6 1.3 %copy-start = (f32[1024,320]{0,1:T(8,128)S(1)}, f32[1024,320]{0,1:T(8,128)}, u32[]{:S(2)}) copy-start(f32[1024,320]{0,1:T(8,128)} %param.12) | copy-start | bytes 3932164
  1.9 1.0 %copy-start.1 = (f32[1024,128]{1,0:T(8,128)S(1)}, f32[1024,128]{1,0:T(8,128)}, u32[]{:S(2)}) copy-start(f32[1024,128]{1,0:T(8,128)} %z_hbm.1) | copy-start | bytes 1572868
  3.0 0.7 %copy-start.2 = (f32[4096]{0:T(1024)S(1)}, f32[4096]{0:T(1024)}, u32[]{:S(2)}) copy-start(f32[4096]{0:T(1024)} %param.9) | copy-start | bytes 49156
  3.7 0.7 %copy-start.3 = (f32[4096]{0:T(1024)S(1)}, f32[4096]{0:T(1024)}, u32[]{:S(2)}) copy-start(f32[4096]{0:T(1024)} %param.10) | copy-start | bytes 49156
  4.4 0.7 %copy-start.4 = (s32[1024,2]{0,1:T(2,128)S(1)}, s32[1024,2]{0,1:T(2,128)}, u32[]{:S(2)}) copy-start(s32[1024,2]{0,1:T(2,128)} %param.15) | copy-start | bytes 24580
  5.1 0.7 %copy-start.5 = (s32[64]{0:T(128)S(1)}, s32[64]{0:T(128)}, u32[]{:S(2)}) copy-start(s32[64]{0:T(128)} %band_next.1) | copy-start | bytes 772
  5.8 0.7 %copy-start.6 = (s32[64]{0:T(128)S(1)}, s32[64]{0:T(128)}, u32[]{:S(2)}) copy-start(s32[64]{0:T(128)} %band_prev.1) | copy-start | bytes 772

commit v3 on v2

--- a/solution.py
+++ b/solution.py
@@ -53,13 +53,14 @@
 
 def kernel(
     sizes,
-    dosage, mean, scale, band_next, ld_hbm, band_prev, z_hbm, observed,
+    dosage, mean_far, scale_far, next_far, ld_far, prev_far, z_far, observed_far,
+    ld_out, imputed_out,
     ld_next, imputed,
-    ld_prev, zscores, seen,
+    mean, scale, band_next, ld_prev, band_prev, zscores, observed, seen,
     dos, dos_side, normed, gram, summed, code_out, code_in, peak_out, peak_in, edge_in,
     vec, vec_two, band_two, image, res1, img0, red,
     in_sem, dos_sem, side_sem, vec_send, vec_recv, red_send, red_recv,
-    code_send, code_recv, peak_send, peak_recv, edge_sem,
+    code_send, code_recv, peak_send, peak_recv, edge_sem, out_sem,
 ):
     n_smp, n_snp, n_pair = sizes
     samples, cols = dos.shape
@@ -83,10 +84,20 @@
     left_id = at_place(jnp.maximum(place - 1, 0))
     right_id = at_place(jnp.minimum(place + 1, places - 1))
 
-    z_fetch = pltpu.make_async_copy(z_hbm, zscores, in_sem.at[0])
-    ld_fetch = pltpu.make_async_copy(ld_hbm, ld_prev, in_sem.at[1])
-    z_fetch.start()
-    ld_fetch.start()
+    small = []
+    for index, (far, near) in enumerate(
+        (
+            (z_far, zscores),
+            (observed_far, observed),
+            (prev_far, band_prev),
+            (ld_far, ld_prev),
+            (mean_far, mean),
+            (scale_far, scale),
+            (next_far, band_next),
+        )
+    ):
+        small.append(pltpu.make_async_copy(far, near, in_sem.at[index]))
+        small[-1].start()
     fetches = []
     for chunk in order:
         span = pl.ds(chunk * CHUNK, CHUNK)
@@ -126,15 +137,6 @@
         @pl.when(me == n_smp - 1)
         def _():
             vec[turn, pl.ds(REACH + rows, REACH), :] = jnp.zeros((REACH, LANES), F32)
-
-    pl.semaphore_wait(
-        barrier,
-        n_smp - 1 + jnp.where(has_left, 1, 0) + jnp.where(has_right, 1, 0),
-    )
-
-    @pl.when(has_left)
-    def _():
-        side_copy.start()
 
     def put_vector(turn, tile, value):
         span = pl.ds(pl.multiple_of(REACH + tile * PAIR, PAIR), PAIR)
@@ -234,7 +236,8 @@
     lane = lax.broadcasted_iota(jnp.int32, (PAIR, LANES), 1)
     line = lax.broadcasted_iota(jnp.int32, (PAIR, LANES), 0)
 
-    z_fetch.wait()
+    small[0].wait()
+    small[1].wait()
     for tile in range(row_blocks):
         here = observed[:, pl.ds(tile * PAIR, PAIR)].astype(F32)
         flags = jnp.zeros((LANES, PAIR), F32)
@@ -244,9 +247,19 @@
         seen[pl.ds(tile * PAIR, PAIR), :] = flags
         put_vector(0, tile, flags * zscores[pl.ds(tile * PAIR, PAIR), :])
 
+    pl.semaphore_wait(
+        barrier,
+        n_smp - 1 + jnp.where(has_left, 1, 0) + jnp.where(has_right, 1, 0),
+    )
+
+    @pl.when(has_left)
+    def _():
+        side_copy.start()
+
     send_halos(0)
 
-    ld_fetch.wait()
+    small[2].wait()
+    small[3].wait()
 
     def two_flags(widths, first_tile, factor):
         left = tile_flags(widths, first_tile, tile_total)
@@ -271,6 +284,9 @@
             band_two[tile, 0:PAIR, third * PAIR : (third + 1) * PAIR] = high
             band_two[tile, PAIR : 2 * PAIR, third * PAIR : (third + 1) * PAIR] = low
 
+    for copy in small[4:]:
+        copy.wait()
+
     def normalise(source, source_col, width, global_col, target_col):
         where = pl.ds(pl.multiple_of(global_col, LANES), width)
         mean_part = mean[:, where]
@@ -540,21 +556,28 @@
 
         lax.fori_loop(0, row_blocks, body, 0)
 
-    middle = (chunks + 1) // 2
-    for chunk in order[:middle]:
+    def make_and_send(chunk):
         make_gram(chunk)
         first_pass_end(chunk)
+
+    middle = (chunks + 1) // 2
+    make_and_send(order[0])
     start_solver()
+    for chunk in order[1:middle]:
+        make_and_send(chunk)
+    scalars0 = next_solver()
     for chunk in order[middle:]:
-        make_gram(chunk)
-        first_pass_end(chunk)
-    scalars0 = next_solver()
-    for chunk in order:
+        make_and_send(chunk)
+    for chunk in order[:middle]:
         first_pass_inner(chunk)
     scalars1 = last_solver(*scalars0)
+    for chunk in order[middle:]:
+        first_pass_inner(chunk)
     for chunk in order[:middle]:
         second_pass(chunk)
     end_solver(scalars0[2], *scalars1)
+    results = [pltpu.make_async_copy(imputed, imputed_out, out_sem.at[blocks])]
+    results[0].start()
 
     inverse = 1.0 / (samples * n_smp)
 
@@ -578,6 +601,11 @@
         for index, flag in enumerate(flags):
             value = jnp.where(lane[0:TILE] < TILE, stack[index], stack[index + 1])
             ld_next[pl.ds(index * TILE, TILE), pl.ds(block * PAIR, PAIR)] = value * flag
+        columns = pl.ds(block * PAIR, PAIR)
+        results.append(
+            pltpu.make_async_copy(ld_next.at[:, columns], ld_out.at[:, columns], out_sem.at[block])
+        )
+        results[-1].start()
 
     done = set()
 
@@ -607,6 +635,9 @@
 
     assemble(0, edge_in[...])
 
+    for copy in results:
+        copy.wait()
+
     @pl.when(has_left)
     def _():
         side_copy.wait_send()
@@ -646,9 +677,7 @@
     chunks = cols // CHUNK
     if traits < LANES:
         zscores = jnp.pad(zscores, ((0, 0), (0, LANES - traits)))
-    vmem = pl.BlockSpec(memory_space=pltpu.VMEM)
-    far = pl.BlockSpec(memory_space=pl.ANY)
-    smem = pl.BlockSpec(memory_space=pltpu.SMEM)
+    far = pl.BlockSpec(memory_space=pltpu.HBM)
     dma = pltpu.SemaphoreType.DMA
     ld_next, imputed = pl.pallas_call(
         functools.partial(kernel, sizes),
@@ -656,13 +685,18 @@
             jax.ShapeDtypeStruct((SPAN * TILE, cols), F32),
             jax.ShapeDtypeStruct((rows, LANES), F32),
         ),
-        in_specs=[
-            far, vmem, vmem, smem, far, smem, far, vmem,
-        ],
-        out_specs=(vmem, vmem),
+        in_specs=[far] * 8,
+        out_specs=(far, far),
         scratch_shapes=[
+            pltpu.VMEM((SPAN * TILE, cols), F32),
+            pltpu.VMEM((rows, LANES), F32),
+            pltpu.VMEM((1, allele_mean.shape[0]), F32),
+            pltpu.VMEM((1, allele_mean.shape[0]), F32),
+            pltpu.SMEM(band_next.shape, jnp.int32),
             pltpu.VMEM((SPAN * TILE, rows), F32),
+            pltpu.SMEM(band_prev.shape, jnp.int32),
             pltpu.VMEM((rows, LANES), F32),
+            pltpu.VMEM((observed.shape[1], rows), jnp.int32),
             pltpu.VMEM((rows, LANES), F32),
             pltpu.VMEM((samples, cols), BF16),
             pltpu.VMEM((samples, REACH), BF16),
@@ -681,7 +715,7 @@
             pltpu.VMEM((rows, LANES), F32),
             pltpu.VMEM((rows, LANES), F32),
             pltpu.VMEM((3, n_smp, 8, LANES), F32),
-            dma((2,)),
+            dma((7,)),
             dma((chunks,)),
             dma((2,)),
             dma((3, 2)),
@@ -693,9 +727,10 @@
             dma((2, chunks)),
             dma((2, chunks)),
             dma((2,)),
+            dma((cols // PAIR + 1,)),
         ],
         compiler_params=pltpu.CompilerParams(
-            collective_id=0, has_side_effects=True, vmem_limit_bytes=48 * 1024 * 1024
+            collective_id=0, has_side_effects=True, vmem_limit_bytes=60 * 1024 * 1024
         ),
     )(
         dosage,

time: 46 us -> 38.2 us (0.83)
  local copies, waits for them, and re-layouts: 7.64 us -> 3.38 us
  Pallas kernels: 37.3 us -> 34 us
    unnamed x16 -> x4, local copies, waits for them, and re-layouts: 7.64 us -> 3.38 us
    pallas_call x1, Pallas kernels: 37.3 us -> 34 us  [local(): pl.pallas_call(functools.partial(kernel, sizes), out_shape=(jax.ShapeDtyp...]
where the time goes in v3:
time: 38.2 us; the launch traced here: 38 us
  Pallas kernels  34 us (89%)
  local copies, waits for them, and re-layouts  3.38 us (9%)
  between operations  0.65 us (2%)
    pallas_call x1, Pallas kernels, local(): pl.pallas_call(functools.partial(kernel, sizes), out_shape=(jax.ShapeDtyp...  34 us
    unnamed x4, local copies, waits for them, and re-layouts  3.38 us

profile of v3, /device:TPU:0, one launch (start us, length us, event | category | flops | bytes accessed | tf_op | source)
XLA Modules:
  0.0 38.0 jit_solution(5536134135585476505)
XLA Ops:
  0.6 34.0 %shard_map.95 = (f32[320,1024]{1,0:T(8,128)}, f32[1024,128]{1,0:T(8,128)}) custom-call(bf16[2048,1024]{1,0:T(8,128)(2,1)} %dosage.1, f32[1,4096]{1,0:T(1,128)} %bitcast.7, f32[1,4096]{1,0:T(1,128)} %bitcast.8, s32[64]{0:T(128)} %next_far.1, f32[320,1024]{1,0:T(8,128)} %bitcast.5, s32[64]{0:T(128)} %prev_far.1, f32[1024,128]{1,0:T(8,128)} %z_far.1, ...), custom_call_target="tpu_custom_call" | custom-call | tf_op jit(solution)/shard_map/pallas_call | solution.py:682
  34.6 0.0 copy-start
  34.6 2.6 %copy.12 = f32[1024,320]{0,1:T(8,128)} copy(f32[1024,320]{0,1:T(8,128)} %bitcast.6) | data formatting | bytes 2621440
  37.2 0.0 copy-done
  37.2 0.8 %copy.13 = f32[1024,128]{1,0:T(8,128)} copy(f32[1024,128]{1,0:T(8,128)S(1)} %copy-done) | data formatting | bytes 1048576
Async XLA Ops:
  34.6 2.6 %copy-start = (f32[1024,128]{1,0:T(8,128)S(1)}, f32[1024,128]{1,0:T(8,128)}, u32[]{:S(2)}) copy-start(f32[1024,128]{1,0:T(8,128)} %get-tuple-element.9) | copy-start | bytes 1572868

commit v4 on v3

--- a/solution.py
+++ b/solution.py
@@ -15,7 +15,7 @@
 LANES = 128
 WIDE = 384
 CHUNK = 256
-STEP = 128
+STEP = 512
 CODE_TOP = 32767.0
 CODE_LEAST = 1e-30
 F32 = jnp.float32
@@ -57,7 +57,7 @@
     ld_out, imputed_out,
     ld_next, imputed,
     mean, scale, band_next, ld_prev, band_prev, zscores, observed, seen,
-    dos, dos_side, normed, gram, summed, code_out, code_in, peak_out, peak_in, edge_in,
+    dos, dos_side, part_own, part_next, gram, summed, code_out, code_in, peak_out, peak_in, edge_in,
     vec, vec_two, band_two, image, res1, img0, red,
     in_sem, dos_sem, side_sem, vec_send, vec_recv, red_send, red_recv,
     code_send, code_recv, peak_send, peak_recv, edge_sem, out_sem,
@@ -287,21 +287,6 @@
     for copy in small[4:]:
         copy.wait()
 
-    def normalise(source, source_col, width, global_col, target_col):
-        where = pl.ds(pl.multiple_of(global_col, LANES), width)
-        mean_part = mean[:, where]
-        scale_part = scale[:, where]
-
-        def body(index, carry):
-            span = pl.ds(pl.multiple_of(index * STEP, STEP), STEP)
-            value = source[span, source_col : source_col + width].astype(F32)
-            normed[span, target_col : target_col + width] = (
-                (value - mean_part) * scale_part
-            ).astype(BF16)
-            return carry
-
-        lax.fori_loop(0, samples // STEP, body, 0)
-
     ready = set()
 
     def make_ready(chunk):
@@ -310,31 +295,55 @@
         ready.add(chunk)
         if chunk < chunks:
             fetches[order.index(chunk)].wait()
-            normalise(dos, chunk * CHUNK, CHUNK, first_col + chunk * CHUNK, chunk * CHUNK)
             return
 
         @pl.when(has_right)
         def _():
             side_copy.wait_recv()
-            normalise(dos_side, 0, REACH, first_col + cols, cols)
 
         @pl.when(jnp.logical_not(has_right))
         def _():
-            normed[:, cols : cols + REACH] = jnp.zeros((samples, REACH), BF16)
+            dos_side[...] = jnp.zeros((samples, REACH), BF16)
+
+    def standards(column, width):
+        column = jnp.minimum(first_col + column, mean.shape[1] - width)
+        where = pl.ds(pl.multiple_of(column, LANES), width)
+        return mean[:, where], scale[:, where]
 
     def make_gram(chunk):
         make_ready(chunk)
         make_ready(chunk + 1)
         low = chunk * CHUNK
-        own = normed[:, low : low + CHUNK]
-        window = normed[:, low : low + CHUNK + REACH]
-        part = lax.dot_general(own, window, (((0,), (0,)), ((), ())), preferred_element_type=F32)
-        first, second = part[0:PAIR, 0:PAIR], part[PAIR:, PAIR : 2 * PAIR]
+        mean_own, scale_own = standards(low, CHUNK)
+        mean_next, scale_next = standards(low + CHUNK, REACH)
+        keep = jnp.where(has_right, 1.0, 0.0) if chunk == chunks - 1 else 1.0
+        scale_next = scale_next * keep
+
+        def body(index, carry):
+            span = pl.ds(pl.multiple_of(index * STEP, STEP), STEP)
+            own = dos[span, low : low + CHUNK].astype(F32)
+            own = ((own - mean_own) * scale_own).astype(BF16)
+            if chunk < chunks - 1:
+                beside = dos[span, low + CHUNK : low + CHUNK + REACH].astype(F32)
+            else:
+                beside = dos_side[span, :].astype(F32)
+            beside = ((beside - mean_next) * scale_next).astype(BF16)
+            dims = (((0,), (0,)), ((), ()))
+            wide = lax.dot_general(own, own, dims, preferred_element_type=F32)
+            late = lax.dot_general(own[:, PAIR:], beside, dims, preferred_element_type=F32)
+            part_own[...] += wide
+            part_next[...] += late
+            return carry
+
+        part_own[...] = jnp.zeros((CHUNK, CHUNK), F32)
+        part_next[...] = jnp.zeros((PAIR, REACH), F32)
+        lax.fori_loop(0, samples // STEP, body, 0)
+        first, second = part_own[0:PAIR, 0:PAIR], part_own[PAIR:, PAIR:]
         gram[chunk, 0] = jnp.where(line <= lane, first, second)
         spare = total_row(jnp.where(line == lane, second, 0.0))
         unused = (line < TILE) & (lane >= TILE)
         for side in range(2):
-            beside = part[side * PAIR : (side + 1) * PAIR, (side + 1) * PAIR : (side + 2) * PAIR]
+            beside = part_own[0:PAIR, PAIR:] if side == 0 else part_next[...]
             held = spare if side == 0 else pltpu.roll(spare, TILE, 1)
             held = jnp.where(line == 0, held, 0.0)
             gram[chunk, 1 + side] = jnp.where(unused, held, beside)
@@ -560,21 +569,23 @@
         make_gram(chunk)
         first_pass_end(chunk)
 
-    middle = (chunks + 1) // 2
     make_and_send(order[0])
     start_solver()
-    for chunk in order[1:middle]:
-        make_and_send(chunk)
+    if chunks > 2:
+        make_and_send(order[1])
+        first_pass_inner(order[0])
     scalars0 = next_solver()
-    for chunk in order[middle:]:
-        make_and_send(chunk)
-    for chunk in order[:middle]:
-        first_pass_inner(chunk)
+    for place_in_order in range(2 if chunks > 2 else 1, chunks):
+        make_and_send(order[place_in_order])
+        first_pass_inner(order[place_in_order - 1])
     scalars1 = last_solver(*scalars0)
-    for chunk in order[middle:]:
-        first_pass_inner(chunk)
-    for chunk in order[:middle]:
-        second_pass(chunk)
+    first_pass_inner(order[-1])
+
+    @pl.when(jnp.logical_not(at_end))
+    def _():
+        for chunk in order:
+            second_pass(chunk)
+
     end_solver(scalars0[2], *scalars1)
     results = [pltpu.make_async_copy(imputed, imputed_out, out_sem.at[blocks])]
     results[0].start()
@@ -617,11 +628,12 @@
                 assemble(block, summed[(block - 1) // 2, 1 + (block - 1) % 2])
 
     assembled = set()
-    for chunk in order[:middle]:
-        done.add(chunk)
-    assemble_ready()
-    for chunk in order[middle:]:
-        second_pass(chunk)
+    for chunk in order:
+
+        @pl.when(at_end)
+        def _():
+            second_pass(chunk)
+
         done.add(chunk)
         assemble_ready()
 
@@ -700,7 +712,8 @@
             pltpu.VMEM((rows, LANES), F32),
             pltpu.VMEM((samples, cols), BF16),
             pltpu.VMEM((samples, REACH), BF16),
-            pltpu.VMEM((samples, cols + REACH), BF16),
+            pltpu.VMEM((CHUNK, CHUNK), F32),
+            pltpu.VMEM((PAIR, REACH), F32),
             pltpu.VMEM((chunks, 3, PAIR, PAIR), F32),
             pltpu.VMEM((chunks, 3, PAIR, PAIR), F32),
             pltpu.VMEM((2, chunks, 3, PAIR, PAIR), jnp.int16),

time: 38.2 us -> 38.3 us (level)
  no operation moved by 1% of the time
where the time goes in v4:
time: 38.3 us; the launch traced here: 38.2 us
  Pallas kernels  34.1 us (89%)
  local copies, waits for them, and re-layouts  3.38 us (9%)
  between operations  0.65 us (2%)
    pallas_call x1, Pallas kernels, local(): pl.pallas_call(functools.partial(kernel, sizes), out_shape=(jax.ShapeDtyp...  34.1 us
    unnamed x4, local copies, waits for them, and re-layouts  3.38 us

profile of v4, /device:TPU:0, one launch (start us, length us, event | category | flops | bytes accessed | tf_op | source)
XLA Modules:
  0.0 38.2 jit_solution(14338816209363927848)
XLA Ops:
  0.6 34.1 %shard_map.95 = (f32[320,1024]{1,0:T(8,128)}, f32[1024,128]{1,0:T(8,128)}) custom-call(bf16[2048,1024]{1,0:T(8,128)(2,1)} %dosage.1, f32[1,4096]{1,0:T(1,128)} %bitcast.7, f32[1,4096]{1,0:T(1,128)} %bitcast.8, s32[64]{0:T(128)} %next_far.1, f32[320,1024]{1,0:T(8,128)} %bitcast.5, s32[64]{0:T(128)} %prev_far.1, f32[1024,128]{1,0:T(8,128)} %z_far.1, ...), custom_call_target="tpu_custom_call" | custom-call | tf_op jit(solution)/shard_map/pallas_call | solution.py:694
  34.8 0.0 copy-start
  34.8 2.6 %copy.12 = f32[1024,320]{0,1:T(8,128)} copy(f32[1024,320]{0,1:T(8,128)} %bitcast.6) | data formatting | bytes 2621440
  37.4 0.0 copy-done
  37.4 0.8 %copy.13 = f32[1024,128]{1,0:T(8,128)} copy(f32[1024,128]{1,0:T(8,128)S(1)} %copy-done) | data formatting | bytes 1048576
Async XLA Ops:
  34.8 2.6 %copy-start = (f32[1024,128]{1,0:T(8,128)S(1)}, f32[1024,128]{1,0:T(8,128)}, u32[]{:S(2)}) copy-start(f32[1024,128]{1,0:T(8,128)} %get-tuple-element.9) | copy-start | bytes 1572868

commit v5 on v4

--- a/solution.py
+++ b/solution.py
@@ -16,6 +16,7 @@
 WIDE = 384
 CHUNK = 256
 STEP = 512
+SIDES = 4
 CODE_TOP = 32767.0
 CODE_LEAST = 1e-30
 F32 = jnp.float32
@@ -57,7 +58,7 @@
     ld_out, imputed_out,
     ld_next, imputed,
     mean, scale, band_next, ld_prev, band_prev, zscores, observed, seen,
-    dos, dos_side, part_own, part_next, gram, summed, code_out, code_in, peak_out, peak_in, edge_in,
+    dos, dos_edge, dos_side, part_own, part_next, gram, summed, code_out, code_in, peak_out, peak_in, edge_in,
     vec, vec_two, band_two, image, res1, img0, red,
     in_sem, dos_sem, side_sem, vec_send, vec_recv, red_send, red_recv,
     code_send, code_recv, peak_send, peak_recv, edge_sem, out_sem,
@@ -84,6 +85,8 @@
     left_id = at_place(jnp.maximum(place - 1, 0))
     right_id = at_place(jnp.minimum(place + 1, places - 1))
 
+    edge_fetch = pltpu.make_async_copy(dosage.at[:, pl.ds(0, REACH)], dos_edge, in_sem.at[7])
+    edge_fetch.start()
     small = []
     for index, (far, near) in enumerate(
         (
@@ -119,24 +122,40 @@
     def _():
         pl.semaphore_signal(barrier, inc=1, device_id=right_id, device_id_type=MESH)
 
-    side_copy = pltpu.make_async_remote_copy(
-        src_ref=dosage.at[:, pl.ds(0, REACH)],
-        dst_ref=dos_side,
-        send_sem=side_sem.at[0],
-        recv_sem=side_sem.at[1],
-        device_id=left_id,
-        device_id_type=MESH,
+    def side_copies():
+        part = samples // SIDES
+        return [
+            pltpu.make_async_remote_copy(
+                src_ref=dos_edge.at[pl.ds(index * part, part)],
+                dst_ref=dos_side.at[pl.ds(index * part, part)],
+                send_sem=side_sem.at[0, index],
+                recv_sem=side_sem.at[1, index],
+                device_id=left_id,
+                device_id_type=MESH,
+            )
+            for index in range(SIDES)
+        ]
+
+    for turn in range(3):
+
+        @pl.when(me == 0)
+        def _():
+            vec[turn, pl.ds(0, REACH), :] = jnp.zeros((REACH, LANES), F32)
+
+        @pl.when(me == n_smp - 1)
+        def _():
+            vec[turn, pl.ds(REACH + rows, REACH), :] = jnp.zeros((REACH, LANES), F32)
+
+    edge_fetch.wait()
+    pl.semaphore_wait(
+        barrier,
+        n_smp - 1 + jnp.where(has_left, 1, 0) + jnp.where(has_right, 1, 0),
     )
 
-    for turn in range(3):
-
-        @pl.when(me == 0)
-        def _():
-            vec[turn, pl.ds(0, REACH), :] = jnp.zeros((REACH, LANES), F32)
-
-        @pl.when(me == n_smp - 1)
-        def _():
-            vec[turn, pl.ds(REACH + rows, REACH), :] = jnp.zeros((REACH, LANES), F32)
+    @pl.when(has_left)
+    def _():
+        for copy in side_copies():
+            copy.start()
 
     def put_vector(turn, tile, value):
         span = pl.ds(pl.multiple_of(REACH + tile * PAIR, PAIR), PAIR)
@@ -246,15 +265,6 @@
         flags = jnp.transpose(flags)
         seen[pl.ds(tile * PAIR, PAIR), :] = flags
         put_vector(0, tile, flags * zscores[pl.ds(tile * PAIR, PAIR), :])
-
-    pl.semaphore_wait(
-        barrier,
-        n_smp - 1 + jnp.where(has_left, 1, 0) + jnp.where(has_right, 1, 0),
-    )
-
-    @pl.when(has_left)
-    def _():
-        side_copy.start()
 
     send_halos(0)
 
@@ -299,7 +309,8 @@
 
         @pl.when(has_right)
         def _():
-            side_copy.wait_recv()
+            for copy in side_copies():
+                copy.wait_recv()
 
         @pl.when(jnp.logical_not(has_right))
         def _():
@@ -652,7 +663,8 @@
 
     @pl.when(has_left)
     def _():
-        side_copy.wait_send()
+        for copy in side_copies():
+            copy.wait_send()
 
     @pl.when(has_right)
     def _():
@@ -712,6 +724,7 @@
             pltpu.VMEM((rows, LANES), F32),
             pltpu.VMEM((samples, cols), BF16),
             pltpu.VMEM((samples, REACH), BF16),
+            pltpu.VMEM((samples, REACH), BF16),
             pltpu.VMEM((CHUNK, CHUNK), F32),
             pltpu.VMEM((PAIR, REACH), F32),
             pltpu.VMEM((chunks, 3, PAIR, PAIR), F32),
@@ -728,9 +741,9 @@
             pltpu.VMEM((rows, LANES), F32),
             pltpu.VMEM((rows, LANES), F32),
             pltpu.VMEM((3, n_smp, 8, LANES), F32),
-            dma((7,)),
+            dma((8,)),
             dma((chunks,)),
-            dma((2,)),
+            dma((2, SIDES)),
             dma((3, 2)),
             dma((3, 2)),
             dma((3, n_smp)),

time: 38.3 us -> 38.5 us (level)
  no operation moved by 1% of the time
where the time goes in v5:
time: 38.5 us; the launch traced here: 38.4 us
  Pallas kernels  34.3 us (89%)
  local copies, waits for them, and re-layouts  3.38 us (9%)
  between operations  0.65 us (2%)
    pallas_call x1, Pallas kernels, local(): pl.pallas_call(functools.partial(kernel, sizes), out_shape=(jax.ShapeDtyp...  34.3 us
    unnamed x4, local copies, waits for them, and re-layouts  3.38 us

profile of v5, /device:TPU:0, one launch (start us, length us, event | category | flops | bytes accessed | tf_op | source)
XLA Modules:
  0.0 38.4 jit_solution(1870891569210702408)
XLA Ops:
  0.6 34.3 %shard_map.95 = (f32[320,1024]{1,0:T(8,128)}, f32[1024,128]{1,0:T(8,128)}) custom-call(bf16[2048,1024]{1,0:T(8,128)(2,1)} %dosage.1, f32[1,4096]{1,0:T(1,128)} %bitcast.7, f32[1,4096]{1,0:T(1,128)} %bitcast.8, s32[64]{0:T(128)} %next_far.1, f32[320,1024]{1,0:T(8,128)} %bitcast.5, s32[64]{0:T(128)} %prev_far.1, f32[1024,128]{1,0:T(8,128)} %z_far.1, ...), custom_call_target="tpu_custom_call" | custom-call | tf_op jit(solution)/shard_map/pallas_call | solution.py:706
  35.0 0.0 copy-start
  35.0 2.6 %copy.12 = f32[1024,320]{0,1:T(8,128)} copy(f32[1024,320]{0,1:T(8,128)} %bitcast.6) | data formatting | bytes 2621440
  37.6 0.0 copy-done
  37.6 0.8 %copy.13 = f32[1024,128]{1,0:T(8,128)} copy(f32[1024,128]{1,0:T(8,128)S(1)} %copy-done) | data formatting | bytes 1048576
Async XLA Ops:
  35.0 2.6 %copy-start = (f32[1024,128]{1,0:T(8,128)S(1)}, f32[1024,128]{1,0:T(8,128)}, u32[]{:S(2)}) copy-start(f32[1024,128]{1,0:T(8,128)} %get-tuple-element.9) | copy-start | bytes 1572868

commit v6 on v5

--- a/solution.py
+++ b/solution.py
@@ -17,6 +17,7 @@
 CHUNK = 256
 STEP = 512
 SIDES = 4
+HANDS = 4
 CODE_TOP = 32767.0
 CODE_LEAST = 1e-30
 F32 = jnp.float32
@@ -75,7 +76,7 @@
     place = lax.axis_index("snp") * n_pair + lax.axis_index("pair")
     places = n_snp * n_pair
     first_col = place * cols
-    order = list(range(1, chunks)) + [0]
+    order = list(range(1, chunks - 1)) + [0, chunks - 1]
 
     def at_place(index):
         return {"snp": index // n_pair, "pair": index % n_pair}
@@ -586,11 +587,13 @@
         make_and_send(order[1])
         first_pass_inner(order[0])
     scalars0 = next_solver()
-    for place_in_order in range(2 if chunks > 2 else 1, chunks):
-        make_and_send(order[place_in_order])
-        first_pass_inner(order[place_in_order - 1])
+    for position in range(2, chunks - 1):
+        make_and_send(order[position])
+        first_pass_inner(order[position - 1])
     scalars1 = last_solver(*scalars0)
-    first_pass_inner(order[-1])
+    make_and_send(order[-1])
+    for chunk in order[-2:]:
+        first_pass_inner(chunk)
 
     @pl.when(jnp.logical_not(at_end))
     def _():
@@ -692,6 +695,21 @@
         def _():
             for copy in running_copies(second_way, chunk):
                 copy.wait_send()
+
+
+def hand_over(ld_held, imputed_held, ld_next, imputed, sems):
+    copies = []
+    for index, (source, target) in enumerate(((ld_held, ld_next), (imputed_held, imputed))):
+        part = source.shape[0] // HANDS
+        for piece in range(HANDS):
+            span = pl.ds(piece * part, part)
+            copies.append(
+                pltpu.make_async_copy(source.at[span], target.at[span], sems.at[index, piece])
+            )
+    for copy in copies:
+        copy.start()
+    for copy in copies:
+        copy.wait()
 
 
 def local(sizes, dosage, allele_mean, snp_scale, band_next, ld_prev, band_prev, zscores, observed):
@@ -768,6 +786,17 @@
         zscores,
         jnp.transpose(observed),
     )
+    ld_next, imputed = pl.pallas_call(
+        hand_over,
+        out_shape=(
+            jax.ShapeDtypeStruct(ld_next.shape, F32),
+            jax.ShapeDtypeStruct(imputed.shape, F32),
+        ),
+        in_specs=[far, far],
+        out_specs=(far, far),
+        scratch_shapes=[dma((2, HANDS))],
+        compiler_params=pltpu.CompilerParams(vmem_limit_bytes=60 * 1024 * 1024),
+    )(ld_next, imputed)
     return jnp.transpose(ld_next), imputed[:, :traits]
 
 

time: 38.5 us -> 92.8 us (2.41)
  Pallas kernels: 34.3 us -> 91.4 us
  local copies, waits for them, and re-layouts: 3.38 us -> 0 us
    pallas_call x0 -> x1, Pallas kernels: none -> 56.8 us  [local(): pl.pallas_call(hand_over, out_shape=(jax.ShapeDtypeStruct(ld_next.shape,...]
    unnamed x4 -> x0, local copies, waits for them, and re-layouts: 3.38 us -> none
where the time goes in v6:
time: 92.8 us; the launch traced here: 92 us
  Pallas kernels  91.4 us (98%)
    pallas_call x1, Pallas kernels, local(): pl.pallas_call(hand_over, out_shape=(jax.ShapeDtypeStruct(ld_next.shape,...  56.8 us
    pallas_call x1, Pallas kernels, local(): pl.pallas_call(functools.partial(kernel, sizes), out_shape=(jax.ShapeDtyp...  34.6 us

profile of v6, /device:TPU:0, one launch (start us, length us, event | category | flops | bytes accessed | tf_op | source)
XLA Modules:
  0.0 92.0 jit_solution(2966662734082210327)
XLA Ops:
  0.6 34.6 %shard_map.95 = (f32[320,1024]{1,0:T(8,128)}, f32[1024,128]{1,0:T(8,128)}) custom-call(bf16[2048,1024]{1,0:T(8,128)(2,1)} %dosage.1, f32[1,4096]{1,0:T(1,128)} %bitcast.6, f32[1,4096]{1,0:T(1,128)} %bitcast.7, s32[64]{0:T(128)} %next_far.1, f32[320,1024]{1,0:T(8,128)} %bitcast.5, s32[64]{0:T(128)} %prev_far.1, f32[1024,128]{1,0:T(8,128)} %z_far.1, ...), custom_call_target="tpu_custom_call" | custom-call | tf_op jit(solution)/shard_map/pallas_call | solution.py:724
  35.3 56.8 %shard_map.96 = (f32[320,1024]{1,0:T(8,128)}, f32[1024,128]{1,0:T(8,128)}) custom-call(f32[320,1024]{1,0:T(8,128)} %get-tuple-element.6.ld_held, f32[1024,128]{1,0:T(8,128)} %get-tuple-element.7.imputed_held), custom_call_target="tpu_custom_call" | custom-call | tf_op jit(solution)/shard_map/pallas_call | solution.py:789

commit v7 on v4

--- a/solution.py
+++ b/solution.py
@@ -16,6 +16,7 @@
 WIDE = 384
 CHUNK = 256
 STEP = 512
+HANDS = 4
 CODE_TOP = 32767.0
 CODE_LEAST = 1e-30
 F32 = jnp.float32
@@ -680,6 +681,26 @@
         def _():
             for copy in running_copies(second_way, chunk):
                 copy.wait_send()
+
+
+def hand_over(ld_held, imputed_held, ld_next, imputed, ld_near, imputed_near, sems):
+    arrays = ((ld_held, ld_near, ld_next), (imputed_held, imputed_near, imputed))
+    inward, outward = [], []
+    for index, (source, near, target) in enumerate(arrays):
+        part = source.shape[0] // HANDS
+        for piece in range(HANDS):
+            span = pl.ds(piece * part, part)
+            sem = sems.at[0, index, piece]
+            inward.append(pltpu.make_async_copy(source.at[span], near.at[span], sem))
+            sem = sems.at[1, index, piece]
+            outward.append(pltpu.make_async_copy(near.at[span], target.at[span], sem))
+    for copy in inward:
+        copy.start()
+    for arrive, leave in zip(inward, outward):
+        arrive.wait()
+        leave.start()
+    for copy in outward:
+        copy.wait()
 
 
 def local(sizes, dosage, allele_mean, snp_scale, band_next, ld_prev, band_prev, zscores, observed):
@@ -755,6 +776,21 @@
         zscores,
         jnp.transpose(observed),
     )
+    ld_next, imputed = pl.pallas_call(
+        hand_over,
+        out_shape=(
+            jax.ShapeDtypeStruct(ld_next.shape, F32),
+            jax.ShapeDtypeStruct(imputed.shape, F32),
+        ),
+        in_specs=[far, far],
+        out_specs=(far, far),
+        scratch_shapes=[
+            pltpu.VMEM(ld_next.shape, F32),
+            pltpu.VMEM(imputed.shape, F32),
+            dma((2, 2, HANDS)),
+        ],
+        compiler_params=pltpu.CompilerParams(vmem_limit_bytes=60 * 1024 * 1024),
+    )(ld_next, imputed)
     return jnp.transpose(ld_next), imputed[:, :traits]
 
 

time: 38.3 us -> 37.3 us (0.974)
  local copies, waits for them, and re-layouts: 3.38 us -> 0 us
  Pallas kernels: 34.1 us -> 36.5 us
    unnamed x4 -> x0, local copies, waits for them, and re-layouts: 3.38 us -> none
    pallas_call x0 -> x1, Pallas kernels: none -> 2.33 us  [local(): pl.pallas_call(hand_over, out_shape=(jax.ShapeDtypeStruct(ld_next.shape,...]
where the time goes in v7:
time: 37.3 us; the launch traced here: 37.1 us
  Pallas kernels  36.5 us (98%)
  between operations  0.64 us (2%)
    pallas_call x1, Pallas kernels, local(): pl.pallas_call(functools.partial(kernel, sizes), out_shape=(jax.ShapeDtyp...  34.1 us
    pallas_call x1, Pallas kernels, local(): pl.pallas_call(hand_over, out_shape=(jax.ShapeDtypeStruct(ld_next.shape,...  2.33 us

profile of v7, /device:TPU:0, one launch (start us, length us, event | category | flops | bytes accessed | tf_op | source)
XLA Modules:
  0.0 37.1 jit_solution(9073146688660560761)
XLA Ops:
  0.6 34.1 %shard_map.95 = (f32[320,1024]{1,0:T(8,128)}, f32[1024,128]{1,0:T(8,128)}) custom-call(bf16[2048,1024]{1,0:T(8,128)(2,1)} %dosage.1, f32[1,4096]{1,0:T(1,128)} %bitcast.6, f32[1,4096]{1,0:T(1,128)} %bitcast.7, s32[64]{0:T(128)} %next_far.1, f32[320,1024]{1,0:T(8,128)} %bitcast.5, s32[64]{0:T(128)} %prev_far.1, f32[1024,128]{1,0:T(8,128)} %z_far.1, ...), custom_call_target="tpu_custom_call" | custom-call | tf_op jit(solution)/shard_map/pallas_call | solution.py:715
  34.8 2.3 %shard_map.96 = (f32[320,1024]{1,0:T(8,128)}, f32[1024,128]{1,0:T(8,128)}) custom-call(f32[320,1024]{1,0:T(8,128)} %get-tuple-element.6.ld_held, f32[1024,128]{1,0:T(8,128)} %get-tuple-element.7.imputed_held), custom_call_target="tpu_custom_call" | custom-call | tf_op jit(solution)/shard_map/pallas_call | solution.py:779
